TPU v7x, 128 devices: a whole 4x4x4 slice. The times are simulated.
128 devices in a mesh: ctx: 32 (over x, z, core), head: 4 (over y).
Axes of the slice: x: 4, y: 4, z: 4, core: 2. Of those that a mesh axis runs over, the one named last changes fastest.
Arguments:
- x_raw: bfloat16 [32768, 8192], P('ctx', 'head'), may hold values from -6 to 6
- z_gate: bfloat16 [32768, 8192], P('ctx', 'head'), may hold values from -6 to 6
- bc_raw: bfloat16 [32768, 256], P('ctx'), may hold values from -6 to 6
- conv_x: bfloat16 [4, 8192], P(None, 'head'), may hold values from -3 to 3
- conv_bc: bfloat16 [4, 256], replicated, may hold values from -3 to 3
- log_decay: float32 [32768, 128], P('ctx', 'head'), may hold values from -1.2 to 0
- step_size: float32 [32768, 128], P('ctx', 'head'), may hold values from 0.0005 to 0.005
- skip_coef: float32 [128], P('head'), may hold values from 0.4 to 6.1
- norm_gain: bfloat16 [8192], P('head'), may hold values from 0.5 to 1.5
- doc_starts: int32 [2], replicated, may hold values from 1 to 32767
Outputs:
- out: bfloat16 [32768, 8192], P('ctx', 'head')
All inputs are finite; a program needn't handle non-finite values.
Results may differ from a plain program's by a relative error of at most 0.009.
Values may be sent and summed in bfloat16 or wider, within the bound.
A program may use at most 192 MiB of HBM per device.

v0:
```python
import jax
import jax.numpy as jnp
from jax import lax
from jax.sharding import PartitionSpec as P

BLOCK = 256


def shifted(value, axis, steps):
    count = lax.axis_size(axis)
    first, last = (max(0, -steps), min(count, count - steps))
    return lax.ppermute(value, axis, [(source, source + steps) for source in range(first, last)])


def entering(part, axis, combine, identity):
    place = lax.axis_index(axis)
    gathered = jax.tree.map(lambda a: lax.all_gather(a, axis), part)
    state = jax.tree.map(lambda a, e: jnp.zeros_like(a) + jnp.asarray(e, a.dtype), part, identity)

    def one(lap, state):
        return combine(
            state, jax.tree.map(lambda a: lax.dynamic_index_in_dim(a, lap, 0, False), gathered)
        )

    return lax.fori_loop(0, place, one, state)


def segment_count(doc_starts, positions):
    return jnp.sum((doc_starts[None, :] <= positions[:, None]).astype(jnp.int32), axis=1)


def causal_conv(extended, tap_table, positions, seg_ext, row_count):
    margin = tap_table.shape[0] - 1
    tap_weights = tap_table.astype(jnp.float32)
    summed = jnp.zeros((row_count, extended.shape[1]), jnp.float32)
    for offset in range(tap_table.shape[0]):
        lower_row = margin - offset
        usable = (positions[lower_row : lower_row + row_count] >= 0) & (
            seg_ext[lower_row : lower_row + row_count] == seg_ext[margin:]
        )
        summed = summed + tap_weights[offset] * extended[lower_row : lower_row + row_count].astype(
            jnp.float32
        ) * usable[:, None].astype(jnp.float32)
    return jax.nn.silu(summed).astype(jnp.bfloat16)


def block_outputs(c_state, b_state, x_heads, log_cum, step_block, seg_block, opened, held_all):
    block_len = seg_block.shape[1]
    lower_tri = jnp.arange(block_len)[:, None] >= jnp.arange(block_len)[None, :]
    scores = jnp.einsum("cin,cjn->cij", c_state, b_state, preferred_element_type=jnp.float32)
    same_doc = lower_tri[None] & (seg_block[:, :, None] == seg_block[:, None, :])
    head_cum = jnp.moveaxis(log_cum, 2, 1)
    log_gaps = head_cum[:, :, :, None] - head_cum[:, :, None, :]
    same_wide = same_doc[:, None]
    mix_weights = jnp.where(
        same_wide, scores[:, None] * jnp.exp(jnp.where(same_wide, log_gaps, 0.0)), 0.0
    ).astype(jnp.bfloat16)
    u_in = (step_block[:, :, :, None] * x_heads.astype(jnp.float32)).astype(jnp.bfloat16)
    intra_part = jnp.einsum(
        "chij,cjhp->cihp", mix_weights, u_in, preferred_element_type=jnp.float32
    )
    entry_decay = jnp.exp(log_cum) * opened[:, :, None]
    inter_part = entry_decay[:, :, :, None] * jnp.einsum(
        "cin,chpn->cihp", c_state.astype(jnp.float32), held_all, precision=lax.Precision.HIGHEST
    )
    return intra_part + inter_part


def per_device(
    x_raw, z_gate, bc_raw, conv_x, conv_bc, log_decay, step_size, skip_coef, norm_gain, doc_starts
):
    tok_count, width = x_raw.shape
    head_count = log_decay.shape[1]
    head_dim = width // head_count
    state_dim = bc_raw.shape[1] // 2
    margin = conv_x.shape[0] - 1
    block_count = tok_count // BLOCK
    device_index = lax.axis_index("ctx")
    first_token = device_index * tok_count
    prev_x, prev_bc = shifted((x_raw[tok_count - margin :], bc_raw[tok_count - margin :]), "ctx", 1)
    positions = first_token - margin + jnp.arange(tok_count + margin, dtype=jnp.int32)
    seg_ext = segment_count(doc_starts, positions)
    seg_tok = seg_ext[margin:]
    conv_out = causal_conv(
        jnp.concatenate([prev_x, x_raw], 0), conv_x, positions, seg_ext, tok_count
    )
    bc_conv = causal_conv(
        jnp.concatenate([prev_bc, bc_raw], 0), conv_bc, positions, seg_ext, tok_count
    )
    b_state = bc_conv[:, :state_dim].reshape(block_count, BLOCK, state_dim)
    c_state = bc_conv[:, state_dim:].reshape(block_count, BLOCK, state_dim)
    x_heads = conv_out.reshape(block_count, BLOCK, head_count, head_dim)
    log_cum = jnp.cumsum(log_decay.reshape(block_count, BLOCK, head_count), axis=1)
    step_block = step_size.reshape(block_count, BLOCK, head_count)
    seg_block = seg_tok.reshape(block_count, BLOCK)
    block_first = first_token + BLOCK * jnp.arange(block_count, dtype=jnp.int32)
    seg_before = segment_count(doc_starts, block_first - 1)
    opened = (seg_block == seg_before[:, None]).astype(jnp.float32)
    closing = (seg_block == seg_block[:, -1:]).astype(jnp.float32)
    to_end = step_block * jnp.exp(log_cum[:, -1:, :] - log_cum) * closing[:, :, None]
    tail_input = (to_end[:, :, :, None] * x_heads.astype(jnp.float32)).astype(jnp.bfloat16)
    fresh_state = jnp.einsum(
        "cshp,csn->chpn", tail_input, b_state, preferred_element_type=jnp.float32
    )
    keep_factor = (
        jnp.exp(log_cum[:, -1, :]) * (seg_block[:, -1] == seg_before).astype(jnp.float32)[:, None]
    )
    running = jnp.zeros((head_count, head_dim, state_dim), jnp.float32)
    entering_list = []
    for block_index in range(block_count):
        entering_list.append(running)
        running = keep_factor[block_index][:, None, None] * running + fresh_state[block_index]
    local_in = jnp.stack(entering_list, 0)
    device_keep = jnp.prod(keep_factor, axis=0)
    enter_decay = jnp.concatenate(
        [jnp.ones((1, head_count), jnp.float32), jnp.cumprod(keep_factor, axis=0)[:-1]], 0
    )

    def combine(earlier_part, later_part):
        return (
            earlier_part[0] * later_part[0],
            later_part[0][:, None, None] * earlier_part[1] + later_part[1],
        )

    prefix = entering(
        (device_keep, running),
        "ctx",
        combine,
        (jnp.ones_like(device_keep), jnp.zeros_like(running)),
    )
    arrived = prefix[1]
    held_all = local_in + enter_decay[:, :, None, None] * arrived[None]
    mixed_out = block_outputs(
        c_state, b_state, x_heads, log_cum, step_block, seg_block, opened, held_all
    )
    summed = mixed_out + skip_coef[None, None, :, None] * x_heads.astype(jnp.float32)
    gated_out = summed.reshape(tok_count, width) * jax.nn.silu(z_gate.astype(jnp.float32))
    local_sq = jnp.sum(gated_out * gated_out, axis=1)
    total_sq = lax.psum(local_sq, "head")
    mean_sq = total_sq / (width * lax.axis_size("head"))
    return (
        gated_out * lax.rsqrt(mean_sq + 1e-05)[:, None] * norm_gain.astype(jnp.float32)[None, :]
    ).astype(jnp.bfloat16)


def solution(mesh):
    in_specs = (
        P("ctx", "head"),
        P("ctx", "head"),
        P("ctx", None),
        P(None, "head"),
        P(),
        P("ctx", "head"),
        P("ctx", "head"),
        P("head"),
        P("head"),
        P(),
    )
    out_specs = P("ctx", "head")
    return jax.shard_map(
        per_device, mesh=mesh, in_specs=in_specs, out_specs=out_specs, check_vma=False
    )
```

profile of v0, /device:TPU:103, one launch (start us, length us, event | category | flops | bytes accessed | tf_op | source)
XLA Modules:
  0.0 329.1 jit_solution(3857443789454757437)
XLA Ops:
  14.6 2.3 reduce-window.6
  21.8 6.4 %copy.74 = bf16[1024,2048]{0,1:T(8,128)(2,1)} copy(bf16[1024,2048]{1,0:T(8,128)(2,1)} %param.12) | data formatting | bytes 8388608 | tf_op args[0]
  29.4 17.4 %fusion.25 = f32[1024,2048]{0,1:T(8,128)} fusion(f32[1024]{0:T(1024)S(1)} %get-tuple-element.77, bf16[1024,2048]{0,1:T(8,128)(2,1)} %copy.74, bf16[3,2048]{0,1:T(8,128)(2,1)S(1)} %collective-permute-done, f32[2048]{0:T(1024)S(1)} %bitcast.95, f32[1024]{0:T(1024)S(1)} %get-tuple-element.78, f32[2048]{0:T(1024)S(1)} %bitcast.94, ...), kind=kLoop, calls=%fused_computation.41 | loop fusion | flops 62914560 | bytes 12644352 | tf_op jit(solution)/shard_map/convert_element_type | solution.py:58
  46.8 10.5 %reshape.150 = f32[4,256,32,64]{1,0,3,2:T(4,128)} reshape(f32[1024,2048]{0,1:T(8,128)} %fusion.25) | data formatting | bytes 16777216 | tf_op jit(solution)/shard_map/convert_element_type | solution.py:58
  57.4 8.7 %multiply_convert_fusion.2 = (bf16[4,256,32,64]{1,0,3,2:T(4,128)(2,1)}, bf16[4,256,32,64]{1,0,3,2:T(4,128)(2,1)S(1)}) fusion(f32[4,256,32,64]{1,0,3,2:T(4,128)} %reshape.150, f32[4,256,32]{1,0,2:T(4,128)S(1)} %mul.339, f32[4,256,32]{1,0,2:T(4,128)S(1)} %get-tuple-element.71), kind=kLoop, calls=%fused_computation.21 | loop fusion | flops 8388608 | bytes 17039360 | tf_op jit(solution)/shard_map/convert_element_type | solution.py:58
  67.4 1.6 slice_add_fusion
  70.6 63.2 %all-reduce.1 = f32[1024]{0:T(1024)S(1)} all-reduce(f32[1024]{0:T(1024)S(1)} %dynamic-update-slice), channel_id=2, replica_groups=mesh['ctx'=32,'head'=4] {'ctx'}, use_global_device_ids=true, to_apply=%add.1 | all-reduce | flops 1024 | bytes 8192
  135.2 6.4 %copy.91 = bf16[1024,2048]{0,1:T(8,128)(2,1)} copy(bf16[1024,2048]{1,0:T(8,128)(2,1)} %param.13) | data formatting | bytes 8388608 | tf_op args[1]
  144.5 41.3 %all-gather.3.cloned.1.call-done = f32[32,32,64,128]{3,2,1,0:T(8,128)} async-done(((f32[1,32,64,128]{3,2,1,0:T(8,128)}), f32[32,32,64,128]{3,2,1,0:T(8,128)}) %all-gather.3.cloned.1.call-update) | async-done | bytes 33554448 | tf_op jit(solution)/shard_map/all_gather | solution.py:17
  185.9 67.0 %while.12 = (s32[]{:T(128)}, f32[32,64,128]{2,1,0:T(8,128)S(1)}, s32[]{:T(128)}, f32[32,32]{1,0:T(8,128)}, f32[32,32,64,128]{3,2,1,0:T(8,128)}, /*index=5*/s32[]{:T(128)}, s32[]{:T(128)}, s32[]{:T(128)}) while((s32[]{:T(128)}, f32[32,64,128]{2,1,0:T(8,128)S(1)}, s32[]{:T(128)}, f32[32,32]{1,0:T(8,128)}, f32[32,32,64,128]{3,2,1,0:T(8,128)}, ...), condition=%wide.region_7.8_spmd, body=%wide.region_6.7_spmd.sunk | while | flops 524293 | bytes 3146239 | solution.py:25
  193.1 1.4 bitcast_add_fusion.3
  195.2 1.4 bitcast_add_fusion.3
  197.4 1.4 bitcast_add_fusion.3
  199.6 1.4 bitcast_add_fusion.3
  208.2 1.4 bitcast_add_fusion.3
  253.0 5.1 %fusion.13 = f32[4,256,32,64]{1,3,2,0:T(8,128)S(1)} fusion(bf16[4,256,128,1]{2,1,3,0:T(8,128)(2,1)S(1)} %bitcast.87, f32[1,32,64,128]{3,2,1,0:T(8,128)S(1)} %get-tuple-element.61, f32[1,32,64,128]{3,2,1,0:T(8,128)S(1)} %get-tuple-element.62, f32[1,32,64,128]{3,2,1,0:T(8,128)} %get-tuple-element.63, f32[4]{0:T(128)} %pad.1.clone, ...), kind=kOutput, calls=%fused_computation.31 | convolution fusion | flops 3226468352 | bytes 12845584 | tf_op jit(solution)/shard_map/cin,chpn->cihp/dot_general | solution.py:63
  258.1 16.4 %fusion.10 = f32[4,256,32,64]{1,3,2,0:T(8,128)} fusion(f32[4,256,32,64]{1,0,3,2:T(4,128)} %reshape.150, f32[4,256,32,64]{1,3,2,0:T(8,128)S(1)} %fusion.13, f32[4,32,256]{2,1,0:T(8,128)S(1)} %copy_bitcast_fusion, f32[4,256,256]{2,1,0:T(8,128)S(1)} %copy-done.5, pred[4,256,256]{2,1,0:T(8,128)(4,1)S(1)} %copy-done.8, ...), kind=kOutput, calls=%fused_computation.16 | convolution fusion | flops 1124073472 | bytes 30933120 | tf_op jit(solution)/shard_map/chij,cjhp->cihp/dot_general | solution.py:59
  274.5 13.8 %copy.90 = f32[4,256,32,64]{1,0,3,2:T(4,128)} copy(f32[4,256,32,64]{1,3,2,0:T(8,128)} %fusion.10) | data formatting | bytes 16777216 | tf_op jit(solution)/shard_map/add | solution.py:136
  288.2 5.6 %copy.98 = f32[256,8,4,256]{3,1,2,0:T(8,128)S(1)} copy(f32[256,8,4,256]{3,2,1,0:T(4,128)} %bitcast.85) | data formatting | bytes 16777216
  293.9 3.2 copy-done
  297.1 2.9 multiply_reduce_fusion
  300.0 8.5 %psum.7 = f32[1024]{0:T(1024)S(1)} all-reduce(f32[1024]{0:T(1024)S(1)} %multiply_reduce_fusion), channel_id=1, replica_groups=mesh['ctx'=32,'head'=4] {'head'}, use_global_device_ids=true, to_apply=%region_9.10 | all-reduce | flops 1024 | bytes 8192 | tf_op jit(solution)/shard_map/psum | solution.py:139
  308.5 7.4 %multiply_convert_fusion = bf16[1024,2048]{0,1:T(8,128)(2,1)} fusion(f32[2048]{0:T(1024)S(1)} %convert_element_type.131, f32[1024]{0:T(1024)S(1)} %add_rsqrt_fusion, f32[1024,2048]{0,1:T(8,128)} %bitcast.84, bf16[1024,2048]{0,1:T(8,128)(2,1)} %copy.91), kind=kLoop, calls=%fused_computation.18 | loop fusion | flops 18874368 | bytes 16789504 | tf_op jit(solution)/shard_map/convert_element_type | solution.py:143
  315.9 6.4 %copy.92 = bf16[1024,2048]{1,0:T(8,128)(2,1)} copy(bf16[1024,2048]{0,1:T(8,128)(2,1)} %multiply_convert_fusion) | data formatting | bytes 8388608 | tf_op jit(solution)/shard_map/convert_element_type | solution.py:143
  (142 shorter events, 79.3 us)
Async XLA Ops:
  6.5 21.7 %copy-start.6 = (bf16[1024,256]{1,0:T(8,128)(2,1)S(1)}, bf16[1024,256]{1,0:T(8,128)(2,1)}, u32[]{:S(2)}) copy-start(bf16[1024,256]{1,0:T(8,128)(2,1)} %param.14) | copy-start | bytes 1572868
  6.5 179.2 %all-gather.3.cloned.1.call-start = ((), (), s32[]{:S(2)}) async-start(), calls=%async_computation | async-start | bytes 34603008 | tf_op jit(solution)/shard_map/all_gather | solution.py:17
  7.7 21.7 %collective-permute-start = (bf16[3,2048]{0,1:T(8,128)(2,1)S(1)}, bf16[3,2048]{0,1:T(8,128)(2,1)S(1)}, u32[]{:S(2)}, u32[]{:S(2)}) collective-permute-start(bf16[3,2048]{0,1:T(8,128)(2,1)S(1)} %copy.75), channel_id=1, source_target_pairs={{0,4},{4,8},{8,12},{12,16},{16,20},{20,24},{24,28},{28,32},{32,36}... | collective-permute-start | bytes 36872 | tf_op jit(solution)/shard_map/ppermute | solution.py:12
  9.7 18.6 %collective-permute-start.1 = (bf16[3,256]{1,0:T(4,128)(2,1)S(1)}, bf16[3,256]{1,0:T(4,128)(2,1)S(1)}, u32[]{:S(2)}, u32[]{:S(2)}) collective-permute-start(bf16[3,256]{1,0:T(4,128)(2,1)S(1)} %slice.156), channel_id=1, source_target_pairs={{0,4},{4,8},{8,12},{12,16},{16,20},{20,24},{24,28},{28,32},{32,36}... | collective-permute-start | bytes 4616 | tf_op jit(solution)/shard_map/ppermute | solution.py:12
  29.4 36.6 %copy-start.3 = (bf16[1024,128]{1,0:T(8,128)(2,1)}, bf16[1024,128]{1,0:T(8,128)(2,1)S(1)}, u32[]{:S(2)}) copy-start(bf16[1024,128]{1,0:T(8,128)(2,1)S(1)} %get-tuple-element.68) | copy-start | bytes 786436
  66.0 1.3 copy-start.11
  66.0 1.3 copy-start.12
  67.3 1.7 copy-start.15
  67.3 3.1 copy-start.13
  67.3 67.2 %copy-start.7 = (f32[4,256,32]{1,0,2:T(4,128)S(1)}, f32[4,256,32]{1,0,2:T(4,128)}, u32[]{:S(2)}) copy-start(f32[4,256,32]{1,0,2:T(4,128)} %get-tuple-element.70) | copy-start | bytes 393220
  67.3 74.3 %copy-start.10 = (bf16[2048]{0:T(1024)(128)(2,1)S(1)}, bf16[2048]{0:T(1024)(128)(2,1)}, u32[]{:S(2)}) copy-start(bf16[2048]{0:T(1024)(128)(2,1)} %param.20) | copy-start | bytes 12292
  67.3 75.8 %copy-start.4 = (bf16[1024,128]{1,0:T(8,128)(2,1)S(1)}, bf16[1024,128]{1,0:T(8,128)(2,1)}, u32[]{:S(2)}) copy-start(bf16[1024,128]{1,0:T(8,128)(2,1)} %copy-done.3) | copy-start | bytes 786436
  252.9 5.2 %copy-start.2 = (bf16[4,256,32,64]{1,0,3,2:T(4,128)(2,1)S(1)}, bf16[4,256,32,64]{1,0,3,2:T(4,128)(2,1)}, u32[]{:S(2)}) copy-start(bf16[4,256,32,64]{1,0,3,2:T(4,128)(2,1)} %get-tuple-element.66) | copy-start | bytes 12582916
  252.9 5.2 %copy-start.5 = (f32[4,256,256]{2,1,0:T(8,128)S(1)}, f32[4,256,256]{2,1,0:T(8,128)}, u32[]{:S(2)}) copy-start(f32[4,256,256]{2,1,0:T(8,128)} %fusion.48) | copy-start | bytes 3145732
  252.9 5.2 %copy-start.8 = (pred[4,256,256]{2,1,0:T(8,128)(4,1)S(1)}, pred[4,256,256]{2,1,0:T(8,128)(4,1)}, u32[]{:S(2)}) copy-start(pred[4,256,256]{2,1,0:T(8,128)(4,1)} %compare_and_fusion) | copy-start | bytes 786436
  252.9 5.2 %copy-start.9 = (f32[4,256,32]{1,2,0:T(8,128)S(1)}, f32[4,256,32]{1,2,0:T(8,128)}, u32[]{:S(2)}) copy-start(f32[4,256,32]{1,2,0:T(8,128)} %copy.84) | copy-start | bytes 393220
  252.9 5.2 %copy-start.14 = (f32[32]{0:T(128)S(1)}, f32[32]{0:T(128)}, u32[]{:S(2)}) copy-start(f32[32]{0:T(128)} %param.19) | copy-start | bytes 388
  288.2 8.9 %copy-start.1 = (bf16[1024,2048]{0,1:T(8,128)(2,1)S(1)}, bf16[1024,2048]{0,1:T(8,128)(2,1)}, u32[]{:S(2)}) copy-start(bf16[1024,2048]{0,1:T(8,128)(2,1)} %copy.91) | copy-start | bytes 12582916
  293.9 3.2 copy-start
Sparse Core Ops, SparseCore 0:
  69.1 116.5 all-gather.2
where the time goes:
time: 333 us; the launch traced here: 329 us
  other arithmetic  91 us (27%)
  local copies, waits for them, and re-layouts  83 us (25%)
  blocking collectives  71.6 us (22%)
  waiting for transfers between devices  41.3 us (12%)
  matrix products  24 us (7%)
  between operations  14.4 us (4%)
    unnamed x1, blocking collectives  63.2 us
    add x31, other arithmetic, combine(): later_part[0][:, None, None] * earlier_part[1] + later_part[1]  44.6 us
    all_gather x1, waiting for transfers between devices, entering(): gathered = jax.tree.map(lambda a: lax.all_gather(a, axis), part)  41.3 us
    unnamed x38, local copies, waits for them, and re-layouts  22.6 us
    mul x31, local copies, waits for them, and re-layouts, combine(): later_part[0][:, None, None] * earlier_part[1] + later_part[1]  21.2 us
    convert_element_type x1, other arithmetic, block_outputs(): x_heads.astype(jnp.float32)  17.4 us
    dot_general x1, matrix products, block_outputs(): jnp.einsum('chij,cjhp->cihp', mix_weights, u_in, preferred_element_type=j...  16.4 us
    add x1, local copies, waits for them, and re-layouts, per_device(): mixed_out + skip_coef[None, None, :, None] * x_heads.astype(jnp.float32)  13.8 us
  transfers between devices with their start and end apart: 3, of which 1 were waited for; matrix products, arithmetic and copies ran while one was open for 9% of the time, Pallas kernels for 0%

commit v1 on v0

v1 whole, which is shorter than its diff:
```python
import functools

import jax
import jax.numpy as jnp
from jax import lax
from jax.experimental import pallas as pl
from jax.experimental.pallas import tpu as pltpu
from jax.sharding import PartitionSpec as P

MESH = pl.DeviceIdType.MESH
F32, BF16 = jnp.float32, jnp.bfloat16
L = 128
W = 256
HALO = 16
KROWS = 16
NN = (((1,), (0,)), ((), ()))
NT = (((1,), (1,)), ((), ()))


def dot(a, b, dims=NN, precision=None):
    return lax.dot_general(a, b, dims, precision=precision, preferred_element_type=F32)


def iota(shape, dim):
    return lax.broadcasted_iota(jnp.int32, shape, dim)


def split2(value):
    high = value.astype(BF16)
    return high, (value - high.astype(F32)).astype(BF16)


def layer_kernel(
    n, y_count, width_all,
    docs_ref, x_ref, z_ref, bc_ref, ld_ref, st_ref, cx_ref, cbc_ref, skip_ref,
    g_ref, rx_ref,
    xs, zs, bcs, lds, sts, xh, bch, es, smat, gmat, btm, cam, a_s, b_s, e_s, rows, rowsx,
    xcs, vs, hs, yl, sz, sp, rp, ap, ain, sq, sqx,
    load_sem, x_sem, z_sem, halo_send, halo_recv, send1, recv1, send2, recv2, send3, recv3,
):
    me = lax.axis_index("ctx")
    my = lax.axis_index("head")
    tokens, width = x_ref.shape
    heads = ld_ref.shape[1]
    chunks, tiles = tokens // L, width // W
    per_tile = 2 * W // 128
    pieces = per_tile * tiles
    ppo = pieces // n
    hd = width // heads
    first = me * tokens
    docs = [docs_ref[i] for i in range(docs_ref.shape[0])]
    tile0 = lax.rem(me * tiles // n, tiles)

    def tile_at(i):
        return lax.rem(tile0 + i, tiles)

    def cols(t):
        return pl.ds(pl.multiple_of(t * W, W), W)

    def x_copy(t):
        return pltpu.make_async_copy(x_ref.at[:, cols(t)], xs.at[:, cols(t)], x_sem.at[t])

    def z_copy(t):
        return pltpu.make_async_copy(z_ref.at[:, cols(t)], zs.at[:, cols(t)], z_sem.at[t])

    small = [
        pltpu.make_async_copy(ld_ref, lds, load_sem.at[0]),
        pltpu.make_async_copy(st_ref, sts, load_sem.at[1]),
        pltpu.make_async_copy(bc_ref, bcs, load_sem.at[2]),
    ]
    for copy in small:
        copy.start()
    for i in range(tiles):
        x_copy(tile_at(i)).start()
    for i in range(tiles):
        z_copy(tile_at(i)).start()

    barrier = pltpu.get_barrier_semaphore()

    def greet(i, carry):
        pl.semaphore_signal(
            barrier, inc=1, device_id={"ctx": lax.rem(me + i, n)}, device_id_type=MESH
        )
        return carry

    lax.fori_loop(1, n, greet, 0)
    for i in range(1, y_count):
        pl.semaphore_signal(
            barrier, inc=1, device_id={"head": lax.rem(my + i, y_count)}, device_id_type=MESH
        )

    es[...] = jnp.where(
        (iota((2 * heads, width), 1) // hd) == (iota((2 * heads, width), 0) & (heads - 1)), 1.0, 0.0
    ).astype(BF16)

    def crossed(low, high):
        hit = None
        for d in docs:
            one = (d > low) & (d <= high)
            hit = one if hit is None else hit | one
        return hit

    def put2(ref, at, value):
        high, low = split2(value)
        ref[at + (slice(None), slice(0, heads))] = high
        ref[at + (slice(None), slice(heads, 2 * heads))] = low

    small[0].wait()
    small[1].wait()
    tri = jnp.where(iota((L, L), 0) >= iota((L, L), 1), 1.0, 0.0)
    rows[...] = jnp.zeros_like(rows)
    base = jnp.zeros((1, heads), F32)
    centers, ends = [], []
    for q in range(chunks):
        at = slice(q * L, (q + 1) * L)
        lc = dot(tri, lds[at, :], precision=lax.Precision.HIGHEST)
        center, end = lc[L // 2 : L // 2 + 1, :], lc[L - 1 : L, :]
        centers.append(center)
        ends.append(end)
        put2(a_s, (q,), jnp.exp(lc - center))
        put2(b_s, (q,), jnp.exp(center - lc) * sts[at, :])
        put2(e_s, (q,), jnp.exp(base + lc))
        base = base + end
    for q in range(chunks):
        later = centers[q + 1] if q + 1 < chunks else jnp.zeros((1, heads), F32)
        k = jnp.exp(ends[q] - centers[q] + later)
        b = jnp.full((1, heads), first + q * L, jnp.int32)
        rows[q : q + 1, :] = jnp.where(crossed(b - 1, b + (L - 1)), 0.0, k)
        rows[chunks + q : chunks + q + 1, :] = k
    b = jnp.full((1, heads), first, jnp.int32)
    rows[2 * chunks : 2 * chunks + 1, :] = jnp.where(
        crossed(b - 1, b + (tokens - 1)), 0.0, jnp.exp(base)
    )
    rows[2 * chunks + 1 : 2 * chunks + 2, :] = skip_ref[...]
    r_high, r_low = split2(rows[...])
    rowsx[...] = dot(r_high, es[0:heads, :]) + dot(r_low, es[0:heads, :])

    t_at = iota((L, L), 0)
    s_at = iota((L, L), 1)
    lag_of = (s_at // HALO) + 1
    from_halo = (s_at - (lag_of - 1) * HALO == t_at + HALO - lag_of) & (s_at < 3 * HALO)
    for q in range(chunks):
        t_all = t_at + (first + q * L)
        for lag in range(1, 4):
            ok = (s_at == t_at - lag) & ~crossed(t_all - lag, t_all)
            smat[q, :, (lag - 1) * L : lag * L] = jnp.where(ok, 1.0, 0.0).astype(BF16)
        ok = from_halo & ~crossed(t_all - lag_of, t_all)
        smat[q, :, 3 * L : 4 * L] = jnp.where(ok, 1.0, 0.0).astype(BF16)

    pl.semaphore_wait(barrier, n - 1 + y_count - 1)

    def halo_copies():
        to = {"ctx": lax.rem(me + 1, n)}
        tail = pl.ds(tokens - HALO, HALO)
        return (
            pltpu.make_async_remote_copy(
                src_ref=x_ref.at[tail, :], dst_ref=xh, send_sem=halo_send.at[0],
                recv_sem=halo_recv.at[0], device_id=to, device_id_type=MESH,
            ),
            pltpu.make_async_remote_copy(
                src_ref=bc_ref.at[tail, :], dst_ref=bch, send_sem=halo_send.at[1],
                recv_sem=halo_recv.at[1], device_id=to, device_id_type=MESH,
            ),
        )

    @pl.when(me < n - 1)
    def _():
        for copy in halo_copies():
            copy.start()

    small[2].wait()

    @pl.when(me == 0)
    def _():
        xh[...] = jnp.zeros_like(xh)
        bch[...] = jnp.zeros_like(bch)

    @pl.when(me > 0)
    def _():
        for copy in halo_copies():
            copy.wait_recv()

    def conv_half(q, block, before, taps):
        taps16 = taps.astype(BF16)
        parts = [block * taps16[lag : lag + 1, :] for lag in range(1, 4)]
        parts += [before * taps16[lag : lag + 1, :] for lag in range(1, 4)]
        parts.append(jnp.zeros((L - 3 * HALO, W), BF16))
        moved = dot(smat[q], jnp.concatenate(parts, axis=0))
        return moved + block.astype(F32) * taps[0:1, :]

    def silu_of_half(half):
        return half + half * jnp.tanh(half)

    taps_bc = cbc_ref[...].astype(F32) * 0.5
    for q in range(chunks):
        block = bcs[q * L : (q + 1) * L, :]
        before = bch[...] if q == 0 else bcs[q * L - HALO : q * L, :]
        both = silu_of_half(conv_half(q, block, before, taps_bc))
        b_st, c_st = both[:, :128], both[:, 128:]
        t_all = t_at + (first + q * L)
        s_all = s_at + (first + q * L)
        b16, c16 = b_st.astype(BF16), c_st.astype(BF16)
        scores = dot(c16, b16, NT)
        ok = (s_at <= t_at) & ~crossed(s_all, t_all)
        gmat[q, :, 0:L] = jnp.where(ok, scores, 0.0).astype(BF16)
        begin = jnp.full((L, L), first + q * L, jnp.int32)
        gmat[q, :, L : 2 * L] = jnp.where(crossed(begin - 1, t_all), 0.0, c_st).astype(BF16)
        begin = jnp.full((L, L), first, jnp.int32)
        cam[q] = jnp.where(crossed(begin - 1, t_all), 0.0, c_st).astype(BF16)
        last = jnp.full((L, L), first + (q + 1) * L - 1, jnp.int32)
        btm[q] = jnp.transpose(jnp.where(crossed(t_all, last), 0.0, b_st)).astype(BF16)

    def piece_copy(p):
        owner = p // ppo
        return pltpu.make_async_remote_copy(
            src_ref=sp.at[p], dst_ref=rp.at[me, lax.rem(p, ppo)], send_sem=send1.at[p],
            recv_sem=recv1.at[me * ppo + lax.rem(p, ppo)],
            device_id={"ctx": owner}, device_id_type=MESH,
        )

    def pass_a(i, carry):
        t = tile_at(i)
        x_copy(t).wait()
        taps = cx_ref[:, cols(t)].astype(F32) * 0.5
        etile = es[:, cols(t)]
        state = jnp.zeros((128, W), F32)
        for q in range(chunks):
            at = slice(q * L, (q + 1) * L)
            block = xs[at, cols(t)]
            before = xh[:, cols(t)] if q == 0 else xs[q * L - HALO : q * L, cols(t)]
            xc = silu_of_half(conv_half(q, block, before, taps))
            xcs[at, cols(t)] = xc.astype(BF16)
            v = (xc * dot(b_s[q], etile)).astype(BF16)
            vs[at, cols(t)] = v
            hs[q, :, cols(t)] = state.astype(BF16)
            fresh = dot(btm[q], v)
            state = (
                rowsx[q : q + 1, cols(t)] * state
                + rowsx[chunks + q : chunks + q + 1, cols(t)] * fresh
            )
        keep = rowsx[2 * chunks : 2 * chunks + 1, cols(t)]
        keep_high = keep.astype(BF16).astype(F32)
        krow = iota((KROWS, W), 0)
        kblock = jnp.where(
            krow == 0, keep_high, jnp.where(krow == 1, keep - keep_high, 0.0)
        ).astype(BF16)
        for j in range(per_tile):
            p = t * per_tile + j
            lanes = slice((j // 2) * 128, (j // 2) * 128 + 128)
            sp[p, 0:64, :] = state[(j % 2) * 64 : (j % 2) * 64 + 64, lanes].astype(BF16)
            sp[p, 64 : 64 + KROWS, :] = kblock[:, lanes]

            @pl.when(p // ppo != me)
            def _():
                piece_copy(p).start()

            @pl.when(p // ppo == me)
            def _():
                rp[me, lax.rem(p, ppo)] = sp[p]

        return carry

    lax.fori_loop(0, tiles, pass_a, 0)

    def pass_b(i, carry):
        t = tile_at(i)
        z_copy(t).wait()
        etile = es[:, cols(t)]
        skip = rowsx[2 * chunks + 1 : 2 * chunks + 2, cols(t)]
        for q in range(chunks):
            at = slice(q * L, (q + 1) * L)
            mixed = dot(gmat[q], jnp.concatenate([vs[at, cols(t)], hs[q, :, cols(t)]], axis=0))
            own = mixed * dot(a_s[q], etile) + skip * xcs[at, cols(t)].astype(F32)
            yl[at, cols(t)] = own
            sz[at, cols(t)] = silu_of_half(zs[at, cols(t)].astype(F32) * 0.5)
        return carry

    split_b = 3
    lax.fori_loop(0, split_b, pass_b, 0)

    def piece_in(d, k):
        return pltpu.make_async_remote_copy(
            src_ref=sp.at[0], dst_ref=rp.at[d, k], send_sem=send1.at[0],
            recv_sem=recv1.at[d * ppo + k], device_id={"ctx": me}, device_id_type=MESH,
        )

    def enter_copy(d, k):
        return pltpu.make_async_remote_copy(
            src_ref=ap.at[d, k], dst_ref=ain.at[me * ppo + k], send_sem=send2.at[d * ppo + k],
            recv_sem=recv2.at[me * ppo + k], device_id={"ctx": d}, device_id_type=MESH,
        )

    def enter_in(p):
        return pltpu.make_async_remote_copy(
            src_ref=ap.at[0, 0], dst_ref=ain.at[p], send_sem=send2.at[0],
            recv_sem=recv2.at[p], device_id={"ctx": p // ppo}, device_id_type=MESH,
        )

    for k in range(ppo):
        def scan(d, state):
            @pl.when(d != me)
            def _():
                piece_in(d, k).wait_recv()

            ap[d, k] = state.astype(BF16)
            piece = rp[d, k].astype(F32)
            return (piece[64:65, :] + piece[65:66, :]) * state + piece[0:64, :]

        lax.fori_loop(0, n, scan, jnp.zeros((64, 128), F32))

        def spread(i, carry):
            enter_copy(lax.rem(me + i, n), k).start()
            return carry

        lax.fori_loop(1, n, spread, 0)
        ain[me * ppo + k] = ap[me, k]

    lax.fori_loop(split_b, tiles, pass_b, 0)

    sq[...] = jnp.zeros_like(sq)

    def pass_c(i, carry):
        t = tile_at(i)
        for j in range(per_tile):
            p = t * per_tile + j

            @pl.when(p // ppo != me)
            def _():
                enter_in(p).wait_recv()

        first_piece = t * per_tile
        entering = jnp.concatenate(
            [
                jnp.concatenate([ain[first_piece + 2 * j], ain[first_piece + 2 * j + 1]], axis=0)
                for j in range(per_tile // 2)
            ],
            axis=1,
        )
        etile = es[:, cols(t)]
        for q in range(chunks):
            at = slice(q * L, (q + 1) * L)
            inter = dot(cam[q], entering) * dot(e_s[q], etile)
            gated = (yl[at, cols(t)] + inter) * sz[at, cols(t)]
            g_ref[at, cols(t)] = gated.astype(BF16)
            squares = gated * gated
            sq[at, :] += squares[:, :128] + squares[:, 128:]
        return carry

    lax.fori_loop(0, tiles, pass_c, 0)

    total = jnp.zeros((8, L), F32)
    for q in range(chunks):
        pick = jnp.where(iota((8, 128), 0) == q, 1.0, 0.0).astype(BF16)
        high, low = split2(sq[q * L : (q + 1) * L, :])
        total = total + dot(pick, high, NT) + dot(pick, low, NT)
    sqx[0] = total

    def sq_copy(i):
        return pltpu.make_async_remote_copy(
            src_ref=sqx.at[0], dst_ref=sqx.at[i], send_sem=send3.at[i - 1],
            recv_sem=recv3.at[i - 1], device_id={"head": lax.rem(my + i, y_count)},
            device_id_type=MESH,
        )

    for i in range(1, y_count):
        sq_copy(i).start()
    for i in range(1, y_count):
        sq_copy(i).wait_recv()
    whole = sqx[0]
    for i in range(1, y_count):
        whole = whole + sqx[i]
    scale = lax.rsqrt(whole * (1.0 / width_all) + 1e-05)
    for q in range(chunks):
        rx_ref[q * L : (q + 1) * L, :] = jnp.transpose(
            jnp.broadcast_to(scale[q : q + 1, :], (128, L))
        )

    for i in range(1, y_count):
        sq_copy(i).wait_send()

    @pl.when(me < n - 1)
    def _():
        for copy in halo_copies():
            copy.wait_send()

    def drain1(p, carry):
        @pl.when(p // ppo != me)
        def _():
            piece_copy(p).wait_send()

        return carry

    lax.fori_loop(0, pieces, drain1, 0)
    for k in range(ppo):
        def drain2(i, carry):
            enter_copy(lax.rem(me + i, n), k).wait_send()
            return carry

        lax.fori_loop(1, n, drain2, 0)


def norm_kernel(g_ref, rx_ref, gain_ref, out_ref):
    rows, width = g_ref.shape
    scale = rx_ref[...]
    for j in range(width // 128):
        at = slice(j * 128, (j + 1) * 128)
        out_ref[:, at] = (
            g_ref[:, at].astype(F32) * scale * gain_ref[:, at].astype(F32)
        ).astype(BF16)


def per_device(
    n, y_count,
    x_raw, z_gate, bc_raw, conv_x, conv_bc, log_decay, step_size, skip_coef, norm_gain, doc_starts,
):
    tokens, width = x_raw.shape
    heads = log_decay.shape[1]
    chunks, tiles = tokens // L, width // W
    pieces = 4 * tiles
    ppo = pieces // n
    any_spec = pl.BlockSpec(memory_space=pl.ANY)
    vmem = pl.BlockSpec(memory_space=pltpu.VMEM)
    smem = pl.BlockSpec(memory_space=pltpu.SMEM)
    dma = pltpu.SemaphoreType.DMA
    gated, scale = pl.pallas_call(
        functools.partial(layer_kernel, n, y_count, float(width * y_count)),
        out_shape=(
            jax.ShapeDtypeStruct((tokens, width), BF16),
            jax.ShapeDtypeStruct((tokens, 128), F32),
        ),
        in_specs=[smem] + [any_spec] * 5 + [vmem] * 3,
        out_specs=(vmem, vmem),
        scratch_shapes=[
            pltpu.VMEM((tokens, width), BF16),
            pltpu.VMEM((tokens, width), BF16),
            pltpu.VMEM((tokens, 256), BF16),
            pltpu.VMEM((tokens, heads), F32),
            pltpu.VMEM((tokens, heads), F32),
            pltpu.VMEM((HALO, width), BF16),
            pltpu.VMEM((HALO, 256), BF16),
            pltpu.VMEM((2 * heads, width), BF16),
            pltpu.VMEM((chunks, L, 4 * L), BF16),
            pltpu.VMEM((chunks, L, 2 * L), BF16),
            pltpu.VMEM((chunks, 128, L), BF16),
            pltpu.VMEM((chunks, L, 128), BF16),
            pltpu.VMEM((chunks, L, 2 * heads), BF16),
            pltpu.VMEM((chunks, L, 2 * heads), BF16),
            pltpu.VMEM((chunks, L, 2 * heads), BF16),
            pltpu.VMEM((32, heads), F32),
            pltpu.VMEM((32, width), F32),
            pltpu.VMEM((tokens, width), BF16),
            pltpu.VMEM((tokens, width), BF16),
            pltpu.VMEM((chunks, 128, width), BF16),
            pltpu.VMEM((tokens, width), F32),
            pltpu.VMEM((tokens, width), F32),
            pltpu.VMEM((pieces, 64 + KROWS, 128), BF16),
            pltpu.VMEM((n, ppo, 64 + KROWS, 128), BF16),
            pltpu.VMEM((n, ppo, 64, 128), BF16),
            pltpu.VMEM((pieces, 64, 128), BF16),
            pltpu.VMEM((tokens, 128), F32),
            pltpu.VMEM((y_count, 8, 128), F32),
            dma((3,)), dma((tiles,)), dma((tiles,)), dma((2,)), dma((2,)),
            dma((pieces,)), dma((pieces,)), dma((pieces,)), dma((pieces,)),
            dma((y_count,)), dma((y_count,)),
        ],
        compiler_params=pltpu.CompilerParams(
            collective_id=0, has_side_effects=True, vmem_limit_bytes=60 * 1024 * 1024
        ),
        name="layer",
    )(
        doc_starts, x_raw, z_gate, bc_raw, log_decay, step_size, conv_x, conv_bc,
        skip_coef.reshape(1, heads),
    )
    block = 256
    return pl.pallas_call(
        norm_kernel,
        out_shape=jax.ShapeDtypeStruct((tokens, width), BF16),
        grid=(tokens // block,),
        in_specs=[
            pl.BlockSpec((block, width), lambda i: (i, 0)),
            pl.BlockSpec((block, 128), lambda i: (i, 0)),
            pl.BlockSpec((1, width), lambda i: (0, 0)),
        ],
        out_specs=pl.BlockSpec((block, width), lambda i: (i, 0)),
        name="norm",
    )(gated, scale, norm_gain.reshape(1, width))


def solution(mesh):
    in_specs = (
        P("ctx", "head"),
        P("ctx", "head"),
        P("ctx", None),
        P(None, "head"),
        P(),
        P("ctx", "head"),
        P("ctx", "head"),
        P("head"),
        P("head"),
        P(),
    )
    return jax.shard_map(
        functools.partial(per_device, mesh.shape["ctx"], mesh.shape["head"]),
        mesh=mesh, in_specs=in_specs, out_specs=P("ctx", "head"), check_vma=False,
    )
```

time: 333 us -> 62.9 us (0.19)
  the two profiles are of different devices: /device:TPU:103 before, /device:TPU:1 now
where the time goes in v1:
time: 62.9 us; the launch traced here: 61.8 us
  Pallas kernels  56.7 us (90%)
  local copies, waits for them, and re-layouts  5.11 us (8%)
    pallas_call x1, Pallas kernels, per_device(): pl.pallas_call(functools.partial(layer_kernel, n, y_count, float(width *...  51.4 us
    pallas_call x1, Pallas kernels, per_device(): pl.pallas_call(norm_kernel, out_shape=jax.ShapeDtypeStruct((tokens, width...  5.3 us
    unnamed x2, local copies, waits for them, and re-layouts  3.82 us
    reshape x1, local copies, waits for them, and re-layouts, per_device(): norm_gain.reshape(1, width)  1.29 us

profile of v1, /device:TPU:1, one launch (start us, length us, event | category | flops | bytes accessed | tf_op | source)
XLA Modules:
  0.0 61.8 jit_solution(6250824705667864676)
XLA Ops:
  0.0 1.3 %reshape.7.gain_ref = bf16[1,2048]{1,0:T(2,128)(2,1)} reshape(bf16[2048]{0:T(1024)(128)(2,1)} %param.18) | data formatting | bytes 8192 | tf_op jit(solution)/shard_map/reshape | solution.py:486
  1.3 1.9 %copy.11.ld_ref = f32[1024,32]{1,0:T(8,128)} copy(f32[1024,32]{0,1:T(8,128)} %param.15) | data formatting | bytes 262144 | tf_op args[5]
  3.2 1.9 %copy.12.st_ref = f32[1024,32]{1,0:T(8,128)} copy(f32[1024,32]{0,1:T(8,128)} %param.16) | data formatting | bytes 262144 | tf_op args[6]
  5.1 51.4 %layer.1 = (bf16[1024,2048]{1,0:T(8,128)(2,1)}, f32[1024,128]{1,0:T(8,128)}) custom-call(s32[2]{0:T(128)} %docs_ref.1, bf16[1024,2048]{1,0:T(8,128)(2,1)} %x_ref.1, bf16[1024,2048]{1,0:T(8,128)(2,1)} %z_ref.1, bf16[1024,256]{1,0:T(8,128)(2,1)} %bc_ref.1, f32[1024,32]{1,0:T(8,128)} %copy.11.ld_ref, f32[1024,32]{1,0:T(8,128)} %copy.12.st_ref, ...), custom_call_target="tpu_custom_call" | custom-call | tf_op jit(solution)/shard_map/layer/pallas_call | solution.py:425
  56.5 5.3 %norm.1 = bf16[1024,2048]{1,0:T(8,128)(2,1)} custom-call(bf16[1024,2048]{1,0:T(8,128)(2,1)} %get-tuple-element.7.g_ref, f32[1024,128]{1,0:T(8,128)} %get-tuple-element.8.rx_ref, bf16[1,2048]{1,0:T(2,128)(2,1)} %reshape.7.gain_ref), custom_call_target="tpu_custom_call" | custom-call | tf_op jit(solution)/shard_map/norm/pallas_call | solution.py:475

commit v2 on v1

--- a/solution.py
+++ b/solution.py
@@ -32,16 +32,16 @@
 
 def layer_kernel(
     n, y_count, width_all,
-    docs_ref, x_ref, z_ref, bc_ref, ld_ref, st_ref, cx_ref, cbc_ref, skip_ref,
+    docs_ref, x_ref, z_ref, bc_ref, ld_ref, st_ref, cx_hbm, cbc_hbm, skip_hbm,
     g_ref, rx_ref,
-    xs, zs, bcs, lds, sts, xh, bch, es, smat, gmat, btm, cam, a_s, b_s, e_s, rows, rowsx,
-    xcs, vs, hs, yl, sz, sp, rp, ap, ain, sq, sqx,
+    xs, zs, bcs, lds, sts, cx_ref, cbc_ref, skip_ref, xh, bch, es, m1, m2, gbm, com, cam, a_s, b_s, e_s, rows, rowsx,
+    xcs, hs, yl, sz, wide, wide2, sp, rp, ap, ain, sq, sqx,
     load_sem, x_sem, z_sem, halo_send, halo_recv, send1, recv1, send2, recv2, send3, recv3,
 ):
     me = lax.axis_index("ctx")
     my = lax.axis_index("head")
     tokens, width = x_ref.shape
-    heads = ld_ref.shape[1]
+    heads = ld_ref.shape[0]
     chunks, tiles = tokens // L, width // W
     per_tile = 2 * W // 128
     pieces = per_tile * tiles
@@ -67,6 +67,9 @@
         pltpu.make_async_copy(ld_ref, lds, load_sem.at[0]),
         pltpu.make_async_copy(st_ref, sts, load_sem.at[1]),
         pltpu.make_async_copy(bc_ref, bcs, load_sem.at[2]),
+        pltpu.make_async_copy(cx_hbm, cx_ref, load_sem.at[3]),
+        pltpu.make_async_copy(cbc_hbm, cbc_ref, load_sem.at[4]),
+        pltpu.make_async_copy(skip_hbm, skip_ref, load_sem.at[5]),
     ]
     for copy in small:
         copy.start()
@@ -100,52 +103,49 @@
             hit = one if hit is None else hit | one
         return hit
 
-    def put2(ref, at, value):
-        high, low = split2(value)
-        ref[at + (slice(None), slice(0, heads))] = high
-        ref[at + (slice(None), slice(heads, 2 * heads))] = low
+    def put2(ref, q, value):
+        high = value.astype(BF16).astype(F32)
+        both = jnp.concatenate([high, value - high], axis=0)
+        ref[q * L : (q + 1) * L, :] = jnp.transpose(both).astype(BF16)
 
     small[0].wait()
     small[1].wait()
-    tri = jnp.where(iota((L, L), 0) >= iota((L, L), 1), 1.0, 0.0)
-    rows[...] = jnp.zeros_like(rows)
-    base = jnp.zeros((1, heads), F32)
+    small[5].wait()
+    tri = jnp.where(iota((L, L), 0) <= iota((L, L), 1), 1.0, 0.0)
+    base = jnp.zeros((heads, 1), F32)
     centers, ends = [], []
     for q in range(chunks):
         at = slice(q * L, (q + 1) * L)
-        lc = dot(tri, lds[at, :], precision=lax.Precision.HIGHEST)
-        center, end = lc[L // 2 : L // 2 + 1, :], lc[L - 1 : L, :]
+        lc = dot(lds[:, at], tri, precision=lax.Precision.HIGHEST)
+        center, end = lc[:, L // 2 : L // 2 + 1], lc[:, L - 1 : L]
         centers.append(center)
         ends.append(end)
-        put2(a_s, (q,), jnp.exp(lc - center))
-        put2(b_s, (q,), jnp.exp(center - lc) * sts[at, :])
-        put2(e_s, (q,), jnp.exp(base + lc))
+        put2(a_s, q, jnp.exp(lc - center))
+        put2(b_s, q, jnp.exp(center - lc) * sts[:, at])
+        put2(e_s, q, jnp.exp(base + lc))
         base = base + end
+    lane = iota((heads, 128), 1)
+    table = jnp.zeros((heads, 128), F32)
     for q in range(chunks):
-        later = centers[q + 1] if q + 1 < chunks else jnp.zeros((1, heads), F32)
+        later = centers[q + 1] if q + 1 < chunks else jnp.zeros((heads, 1), F32)
         k = jnp.exp(ends[q] - centers[q] + later)
-        b = jnp.full((1, heads), first + q * L, jnp.int32)
-        rows[q : q + 1, :] = jnp.where(crossed(b - 1, b + (L - 1)), 0.0, k)
-        rows[chunks + q : chunks + q + 1, :] = k
-    b = jnp.full((1, heads), first, jnp.int32)
-    rows[2 * chunks : 2 * chunks + 1, :] = jnp.where(
-        crossed(b - 1, b + (tokens - 1)), 0.0, jnp.exp(base)
-    )
+        b = jnp.full((heads, 1), first + q * L, jnp.int32)
+        table = jnp.where(lane == q, jnp.where(crossed(b - 1, b + (L - 1)), 0.0, k), table)
+        table = jnp.where(lane == chunks + q, k, table)
+    b = jnp.full((heads, 1), first, jnp.int32)
+    keep_all = jnp.where(crossed(b - 1, b + (tokens - 1)), 0.0, jnp.exp(base))
+    table = jnp.where(lane == 2 * chunks, keep_all, table)
+    rows[...] = jnp.transpose(table)[0:32, :]
     rows[2 * chunks + 1 : 2 * chunks + 2, :] = skip_ref[...]
     r_high, r_low = split2(rows[...])
     rowsx[...] = dot(r_high, es[0:heads, :]) + dot(r_low, es[0:heads, :])
 
+    t_all = iota((HALO + tokens, 128), 0) + (first - HALO)
+    m1[...] = jnp.where(crossed(t_all - 1, t_all), 0.0, 1.0)
+    t_all = iota((tokens, 128), 0) + first
+    m2[...] = jnp.where(crossed(t_all - 2, t_all), 0.0, 1.0)
     t_at = iota((L, L), 0)
     s_at = iota((L, L), 1)
-    lag_of = (s_at // HALO) + 1
-    from_halo = (s_at - (lag_of - 1) * HALO == t_at + HALO - lag_of) & (s_at < 3 * HALO)
-    for q in range(chunks):
-        t_all = t_at + (first + q * L)
-        for lag in range(1, 4):
-            ok = (s_at == t_at - lag) & ~crossed(t_all - lag, t_all)
-            smat[q, :, (lag - 1) * L : lag * L] = jnp.where(ok, 1.0, 0.0).astype(BF16)
-        ok = from_halo & ~crossed(t_all - lag_of, t_all)
-        smat[q, :, 3 * L : 4 * L] = jnp.where(ok, 1.0, 0.0).astype(BF16)
 
     pl.semaphore_wait(barrier, n - 1 + y_count - 1)
 
@@ -169,6 +169,42 @@
             copy.start()
 
     small[2].wait()
+    small[3].wait()
+    small[4].wait()
+
+    def conv_half(q, block, before, taps):
+        ext = jnp.concatenate([before, block], axis=0).astype(F32)
+        mask1 = m1[q * L : q * L + HALO + L, :]
+        mask2 = m2[q * L : (q + 1) * L, :]
+        ext1 = pltpu.roll(ext, 1, 0) * jnp.concatenate([mask1, mask1], axis=1)
+        near = taps[0:1, :] * ext[HALO:] + taps[1:2, :] * ext1[HALO:]
+        far = taps[2:3, :] * ext[8:] + taps[3:4, :] * ext1[8:]
+        far = pltpu.roll(far, 2, 0)[8:]
+        return near + far * jnp.concatenate([mask2, mask2], axis=1)
+
+    def silu_of_half(half):
+        return half + half * jnp.tanh(half)
+
+    taps_bc = cbc_ref[...].astype(F32) * 0.5
+
+    def shared(q, before):
+        block = bcs[q * L : (q + 1) * L, :]
+        both = silu_of_half(conv_half(q, block, before, taps_bc))
+        b_st, c_st = both[:, :128], both[:, 128:]
+        t_all = t_at + (first + q * L)
+        s_all = s_at + (first + q * L)
+        scores = dot(c_st.astype(BF16), b_st.astype(BF16), NT)
+        ok = (s_at <= t_at) & ~crossed(s_all, t_all)
+        gbm[q, 0:L, :] = jnp.where(ok, scores, 0.0).astype(BF16)
+        last = jnp.full((L, L), first + (q + 1) * L - 1, jnp.int32)
+        gbm[q, L : 2 * L, :] = jnp.transpose(jnp.where(crossed(t_all, last), 0.0, b_st)).astype(BF16)
+        begin = jnp.full((L, L), first + q * L, jnp.int32)
+        com[q] = jnp.where(crossed(begin - 1, t_all), 0.0, c_st).astype(BF16)
+        begin = jnp.full((L, L), first, jnp.int32)
+        cam[q * L : (q + 1) * L, :] = jnp.where(crossed(begin - 1, t_all), 0.0, c_st).astype(BF16)
+
+    for q in range(1, chunks):
+        shared(q, bcs[q * L - HALO : q * L, :])
 
     @pl.when(me == 0)
     def _():
@@ -180,35 +216,7 @@
         for copy in halo_copies():
             copy.wait_recv()
 
-    def conv_half(q, block, before, taps):
-        taps16 = taps.astype(BF16)
-        parts = [block * taps16[lag : lag + 1, :] for lag in range(1, 4)]
-        parts += [before * taps16[lag : lag + 1, :] for lag in range(1, 4)]
-        parts.append(jnp.zeros((L - 3 * HALO, W), BF16))
-        moved = dot(smat[q], jnp.concatenate(parts, axis=0))
-        return moved + block.astype(F32) * taps[0:1, :]
-
-    def silu_of_half(half):
-        return half + half * jnp.tanh(half)
-
-    taps_bc = cbc_ref[...].astype(F32) * 0.5
-    for q in range(chunks):
-        block = bcs[q * L : (q + 1) * L, :]
-        before = bch[...] if q == 0 else bcs[q * L - HALO : q * L, :]
-        both = silu_of_half(conv_half(q, block, before, taps_bc))
-        b_st, c_st = both[:, :128], both[:, 128:]
-        t_all = t_at + (first + q * L)
-        s_all = s_at + (first + q * L)
-        b16, c16 = b_st.astype(BF16), c_st.astype(BF16)
-        scores = dot(c16, b16, NT)
-        ok = (s_at <= t_at) & ~crossed(s_all, t_all)
-        gmat[q, :, 0:L] = jnp.where(ok, scores, 0.0).astype(BF16)
-        begin = jnp.full((L, L), first + q * L, jnp.int32)
-        gmat[q, :, L : 2 * L] = jnp.where(crossed(begin - 1, t_all), 0.0, c_st).astype(BF16)
-        begin = jnp.full((L, L), first, jnp.int32)
-        cam[q] = jnp.where(crossed(begin - 1, t_all), 0.0, c_st).astype(BF16)
-        last = jnp.full((L, L), first + (q + 1) * L - 1, jnp.int32)
-        btm[q] = jnp.transpose(jnp.where(crossed(t_all, last), 0.0, b_st)).astype(BF16)
+    shared(0, bch[...])
 
     def piece_copy(p):
         owner = p // ppo
@@ -224,16 +232,18 @@
         taps = cx_ref[:, cols(t)].astype(F32) * 0.5
         etile = es[:, cols(t)]
         state = jnp.zeros((128, W), F32)
+        wide[...] = dot(b_s[...], etile)
         for q in range(chunks):
             at = slice(q * L, (q + 1) * L)
             block = xs[at, cols(t)]
             before = xh[:, cols(t)] if q == 0 else xs[q * L - HALO : q * L, cols(t)]
             xc = silu_of_half(conv_half(q, block, before, taps))
             xcs[at, cols(t)] = xc.astype(BF16)
-            v = (xc * dot(b_s[q], etile)).astype(BF16)
-            vs[at, cols(t)] = v
+            v = (xc * wide[at, :]).astype(BF16)
             hs[q, :, cols(t)] = state.astype(BF16)
-            fresh = dot(btm[q], v)
+            both = dot(gbm[q], v)
+            yl[at, cols(t)] = both[0:L, :]
+            fresh = both[L:, :]
             state = (
                 rowsx[q : q + 1, cols(t)] * state
                 + rowsx[chunks + q : chunks + q + 1, cols(t)] * fresh
@@ -267,10 +277,11 @@
         z_copy(t).wait()
         etile = es[:, cols(t)]
         skip = rowsx[2 * chunks + 1 : 2 * chunks + 2, cols(t)]
+        wide[...] = dot(a_s[...], etile)
         for q in range(chunks):
             at = slice(q * L, (q + 1) * L)
-            mixed = dot(gmat[q], jnp.concatenate([vs[at, cols(t)], hs[q, :, cols(t)]], axis=0))
-            own = mixed * dot(a_s[q], etile) + skip * xcs[at, cols(t)].astype(F32)
+            mixed = yl[at, cols(t)] + dot(com[q], hs[q, :, cols(t)])
+            own = mixed * wide[at, :] + skip * xcs[at, cols(t)].astype(F32)
             yl[at, cols(t)] = own
             sz[at, cols(t)] = silu_of_half(zs[at, cols(t)].astype(F32) * 0.5)
         return carry
@@ -337,10 +348,11 @@
             axis=1,
         )
         etile = es[:, cols(t)]
+        wide[...] = dot(e_s[...], etile)
+        wide2[...] = dot(cam[...], entering)
         for q in range(chunks):
             at = slice(q * L, (q + 1) * L)
-            inter = dot(cam[q], entering) * dot(e_s[q], etile)
-            gated = (yl[at, cols(t)] + inter) * sz[at, cols(t)]
+            gated = (yl[at, cols(t)] + wide2[at, :] * wide[at, :]) * sz[at, cols(t)]
             g_ref[at, cols(t)] = gated.astype(BF16)
             squares = gated * gated
             sq[at, :] += squares[:, :128] + squares[:, 128:]
@@ -399,14 +411,24 @@
         lax.fori_loop(1, n, drain2, 0)
 
 
-def norm_kernel(g_ref, rx_ref, gain_ref, out_ref):
+def norm_kernel(g_ref, rx_ref, gain_ref, out_ref, stage, sem):
     rows, width = g_ref.shape
-    scale = rx_ref[...]
-    for j in range(width // 128):
-        at = slice(j * 128, (j + 1) * 128)
-        out_ref[:, at] = (
-            g_ref[:, at].astype(F32) * scale * gain_ref[:, at].astype(F32)
-        ).astype(BF16)
+    block = 128
+    gain = gain_ref[...].reshape(1, width).astype(F32)
+
+    def copy(i):
+        at = pl.ds(i * block, block)
+        return pltpu.make_async_copy(stage.at[at, :], out_ref.at[at, :], sem.at[i])
+
+    for i in range(rows // block):
+        at = slice(i * block, (i + 1) * block)
+        scale = rx_ref[at, :]
+        for j in range(width // 128):
+            lanes = slice(j * 128, (j + 1) * 128)
+            stage[at, lanes] = (g_ref[at, lanes].astype(F32) * scale * gain[:, lanes]).astype(BF16)
+        copy(i).start()
+    for i in range(rows // block):
+        copy(i).wait()
 
 
 def per_device(
@@ -425,65 +447,66 @@
     gated, scale = pl.pallas_call(
         functools.partial(layer_kernel, n, y_count, float(width * y_count)),
         out_shape=(
-            jax.ShapeDtypeStruct((tokens, width), BF16),
-            jax.ShapeDtypeStruct((tokens, 128), F32),
+            pltpu.VMEM((tokens, width), BF16),
+            pltpu.VMEM((tokens, 128), F32),
         ),
-        in_specs=[smem] + [any_spec] * 5 + [vmem] * 3,
+        in_specs=[smem] + [any_spec] * 8,
         out_specs=(vmem, vmem),
         scratch_shapes=[
             pltpu.VMEM((tokens, width), BF16),
             pltpu.VMEM((tokens, width), BF16),
             pltpu.VMEM((tokens, 256), BF16),
-            pltpu.VMEM((tokens, heads), F32),
-            pltpu.VMEM((tokens, heads), F32),
+            pltpu.VMEM((heads, tokens), F32),
+            pltpu.VMEM((heads, tokens), F32),
+            pltpu.VMEM((4, width), BF16),
+            pltpu.VMEM((4, 256), BF16),
+            pltpu.VMEM((1, heads), F32),
             pltpu.VMEM((HALO, width), BF16),
             pltpu.VMEM((HALO, 256), BF16),
             pltpu.VMEM((2 * heads, width), BF16),
-            pltpu.VMEM((chunks, L, 4 * L), BF16),
-            pltpu.VMEM((chunks, L, 2 * L), BF16),
-            pltpu.VMEM((chunks, 128, L), BF16),
+            pltpu.VMEM((HALO + tokens, 128), F32),
+            pltpu.VMEM((tokens, 128), F32),
+            pltpu.VMEM((chunks, 2 * L, L), BF16),
             pltpu.VMEM((chunks, L, 128), BF16),
-            pltpu.VMEM((chunks, L, 2 * heads), BF16),
-            pltpu.VMEM((chunks, L, 2 * heads), BF16),
-            pltpu.VMEM((chunks, L, 2 * heads), BF16),
+            pltpu.VMEM((tokens, 128), BF16),
+            pltpu.VMEM((tokens, 2 * heads), BF16),
+            pltpu.VMEM((tokens, 2 * heads), BF16),
+            pltpu.VMEM((tokens, 2 * heads), BF16),
             pltpu.VMEM((32, heads), F32),
             pltpu.VMEM((32, width), F32),
-            pltpu.VMEM((tokens, width), BF16),
             pltpu.VMEM((tokens, width), BF16),
             pltpu.VMEM((chunks, 128, width), BF16),
             pltpu.VMEM((tokens, width), F32),
             pltpu.VMEM((tokens, width), F32),
+            pltpu.VMEM((tokens, W), F32),
+            pltpu.VMEM((tokens, W), F32),
             pltpu.VMEM((pieces, 64 + KROWS, 128), BF16),
             pltpu.VMEM((n, ppo, 64 + KROWS, 128), BF16),
             pltpu.VMEM((n, ppo, 64, 128), BF16),
             pltpu.VMEM((pieces, 64, 128), BF16),
             pltpu.VMEM((tokens, 128), F32),
             pltpu.VMEM((y_count, 8, 128), F32),
-            dma((3,)), dma((tiles,)), dma((tiles,)), dma((2,)), dma((2,)),
+            dma((6,)), dma((tiles,)), dma((tiles,)), dma((2,)), dma((2,)),
             dma((pieces,)), dma((pieces,)), dma((pieces,)), dma((pieces,)),
             dma((y_count,)), dma((y_count,)),
         ],
         compiler_params=pltpu.CompilerParams(
-            collective_id=0, has_side_effects=True, vmem_limit_bytes=60 * 1024 * 1024
+            collective_id=0, has_side_effects=True, vmem_limit_bytes=59 * 1024 * 1024
         ),
         name="layer",
     )(
-        doc_starts, x_raw, z_gate, bc_raw, log_decay, step_size, conv_x, conv_bc,
+        doc_starts, x_raw, z_gate, bc_raw, log_decay.T, step_size.T, conv_x, conv_bc,
         skip_coef.reshape(1, heads),
     )
-    block = 256
     return pl.pallas_call(
         norm_kernel,
         out_shape=jax.ShapeDtypeStruct((tokens, width), BF16),
-        grid=(tokens // block,),
-        in_specs=[
-            pl.BlockSpec((block, width), lambda i: (i, 0)),
-            pl.BlockSpec((block, 128), lambda i: (i, 0)),
-            pl.BlockSpec((1, width), lambda i: (0, 0)),
-        ],
-        out_specs=pl.BlockSpec((block, width), lambda i: (i, 0)),
+        in_specs=[vmem] * 3,
+        out_specs=any_spec,
+        scratch_shapes=[pltpu.VMEM((tokens, width), BF16), dma((tokens // 128,))],
+        compiler_params=pltpu.CompilerParams(vmem_limit_bytes=16 * 1024 * 1024),
         name="norm",
-    )(gated, scale, norm_gain.reshape(1, width))
+    )(gated, scale, norm_gain)
 
 
 def solution(mesh):

time: 62.9 us -> 45.6 us (0.72); the launches traced: 61.8 us -> 45.2 us
  Pallas kernels: 56.7 us -> 45.2 us
  local copies, waits for them, and re-layouts: 5.11 us -> 0.01 us
    pallas_call x1, Pallas kernels: 51.4 us -> 43 us  [per_device(): pl.pallas_call(functools.partial(layer_kernel, n, y_count, float(width *...]
    unnamed x2, local copies, waits for them, and re-layouts: 3.82 us -> 0.01 us
    pallas_call x1, Pallas kernels: 5.3 us -> 2.25 us  [per_device(): pl.pallas_call(norm_kernel, out_shape=jax.ShapeDtypeStruct((tokens, width...]
    reshape x1 -> x0, local copies, waits for them, and re-layouts: 1.29 us -> none  [per_device(): norm_gain.reshape(1, width)]
where the time goes in v2:
time: 45.6 us; the launch traced here: 45.2 us
  Pallas kernels  45.2 us (99%)
    pallas_call x1, Pallas kernels, per_device(): pl.pallas_call(functools.partial(layer_kernel, n, y_count, float(width *...  43 us
    pallas_call x1, Pallas kernels, per_device(): pl.pallas_call(norm_kernel, out_shape=jax.ShapeDtypeStruct((tokens, width...  2.25 us

profile of v2, /device:TPU:1, one launch (start us, length us, event | category | flops | bytes accessed | tf_op | source)
XLA Modules:
  0.0 45.2 jit_solution(17826998632825900578)
XLA Ops:
  0.0 0.0 copy-start
  0.0 43.0 %layer.1 = (bf16[1024,2048]{1,0:T(8,128)(2,1)S(1)}, f32[1024,128]{1,0:T(8,128)S(1)}) custom-call(s32[2]{0:T(128)} %docs_ref.1, bf16[1024,2048]{1,0:T(8,128)(2,1)} %x_ref.1, bf16[1024,2048]{1,0:T(8,128)(2,1)} %z_ref.1, bf16[1024,256]{1,0:T(8,128)(2,1)} %bc_ref.1, f32[32,1024]{1,0:T(8,128)} %bitcast.3, f32[32,1024]{1,0:T(8,128)} %bitcast.4, ...), custom_call_target="tpu_custom_call" | custom-call | tf_op jit(solution)/shard_map/layer/pallas_call | solution.py:447
  43.0 0.0 copy-done
  43.0 2.2 %norm.1 = bf16[1024,2048]{1,0:T(8,128)(2,1)} custom-call(bf16[1024,2048]{1,0:T(8,128)(2,1)S(1)} %get-tuple-element.7.g_ref, f32[1024,128]{1,0:T(8,128)S(1)} %get-tuple-element.8.rx_ref, bf16[2048]{0:T(1024)(128)(2,1)S(1)} %copy-done), custom_call_target="tpu_custom_call" | custom-call | tf_op jit(solution)/shard_map/norm/pallas_call | solution.py:501
Async XLA Ops:
  0.0 43.0 %copy-start = (bf16[2048]{0:T(1024)(128)(2,1)S(1)}, bf16[2048]{0:T(1024)(128)(2,1)}, u32[]{:S(2)}) copy-start(bf16[2048]{0:T(1024)(128)(2,1)} %gain_ref.1) | copy-start | bytes 12292

commit v3 on v2

--- a/solution.py
+++ b/solution.py
@@ -35,21 +35,26 @@
     docs_ref, x_ref, z_ref, bc_ref, ld_ref, st_ref, cx_hbm, cbc_hbm, skip_hbm,
     g_ref, rx_ref,
     xs, zs, bcs, lds, sts, cx_ref, cbc_ref, skip_ref, xh, bch, es, m1, m2, gbm, com, cam, a_s, b_s, e_s, rows, rowsx,
-    xcs, hs, yl, sz, wide, wide2, sp, rp, ap, ain, sq, sqx,
-    load_sem, x_sem, z_sem, halo_send, halo_recv, send1, recv1, send2, recv2, send3, recv3,
+    xcs, hs, yl, sz, wide, wide2, sp, ex, sc, rp, ap, ain, fw, ent, sq, sqx,
+    load_sem, x_sem, z_sem, halo_send, halo_recv, ex_send, ex_recv, send1, recv1, send2, recv2,
+    fw_send, fw_recv, send3, recv3,
 ):
     me = lax.axis_index("ctx")
     my = lax.axis_index("head")
     tokens, width = x_ref.shape
     heads = ld_ref.shape[0]
     chunks, tiles = tokens // L, width // W
-    per_tile = 2 * W // 128
-    pieces = per_tile * tiles
-    ppo = pieces // n
+    pairs = width // 128
+    per_tile = W // 128
+    chips = n // 2
+    ppc = pairs // chips
+    chip, core = me // 2, lax.rem(me, 2)
+    peer = me + 1 - 2 * core
+    own_rows = pl.ds(pl.multiple_of(core * 64, 64), 64)
     hd = width // heads
     first = me * tokens
     docs = [docs_ref[i] for i in range(docs_ref.shape[0])]
-    tile0 = lax.rem(me * tiles // n, tiles)
+    tile0 = lax.rem(chip * tiles // chips, tiles)
 
     def tile_at(i):
         return lax.rem(tile0 + i, tiles)
@@ -62,6 +67,18 @@
 
     def z_copy(t):
         return pltpu.make_async_copy(z_ref.at[:, cols(t)], zs.at[:, cols(t)], z_sem.at[t])
+
+    barrier = pltpu.get_barrier_semaphore()
+
+    def greet(device):
+        pl.semaphore_signal(barrier, inc=1, device_id=device, device_id_type=MESH)
+
+    greet({"ctx": peer})
+    greet({"ctx": lax.rem(me + n - 1 + 2 * core, n)})
+    for i in range(1, chips):
+        greet({"ctx": lax.rem(me + 2 * i, n)})
+    for i in range(1, y_count):
+        greet({"head": lax.rem(my + i, y_count)})
 
     small = [
         pltpu.make_async_copy(ld_ref, lds, load_sem.at[0]),
@@ -78,20 +95,6 @@
     for i in range(tiles):
         z_copy(tile_at(i)).start()
 
-    barrier = pltpu.get_barrier_semaphore()
-
-    def greet(i, carry):
-        pl.semaphore_signal(
-            barrier, inc=1, device_id={"ctx": lax.rem(me + i, n)}, device_id_type=MESH
-        )
-        return carry
-
-    lax.fori_loop(1, n, greet, 0)
-    for i in range(1, y_count):
-        pl.semaphore_signal(
-            barrier, inc=1, device_id={"head": lax.rem(my + i, y_count)}, device_id_type=MESH
-        )
-
     es[...] = jnp.where(
         (iota((2 * heads, width), 1) // hd) == (iota((2 * heads, width), 0) & (heads - 1)), 1.0, 0.0
     ).astype(BF16)
@@ -103,27 +106,57 @@
             hit = one if hit is None else hit | one
         return hit
 
-    def put2(ref, q, value):
+    def put2(ref, value):
         high = value.astype(BF16).astype(F32)
-        both = jnp.concatenate([high, value - high], axis=0)
-        ref[q * L : (q + 1) * L, :] = jnp.transpose(both).astype(BF16)
+        low = value - high
+        for q in range(chunks):
+            at = slice(q * heads, (q + 1) * heads)
+            both = jnp.concatenate([high[at], low[at]], axis=0)
+            ref[q * L : (q + 1) * L, :] = jnp.transpose(both).astype(BF16)
 
     small[0].wait()
     small[1].wait()
     small[5].wait()
-    tri = jnp.where(iota((L, L), 0) <= iota((L, L), 1), 1.0, 0.0)
-    base = jnp.zeros((heads, 1), F32)
-    centers, ends = [], []
+    tri = jnp.where(iota((L, L), 0) <= iota((L, L), 1), 1.0, 0.0).astype(BF16)
+    ld = jnp.concatenate([lds[:, q * L : (q + 1) * L] for q in range(chunks)], axis=0)
+    st = jnp.concatenate([sts[:, q * L : (q + 1) * L] for q in range(chunks)], axis=0)
+    high, mid = split2(ld)
+    low = (ld - high.astype(F32) - mid.astype(F32)).astype(BF16)
+    sums = dot(jnp.concatenate([high, mid, low], axis=0), tri)
+    rows_all = chunks * heads
+    lc = sums[0:rows_all] + (sums[rows_all : 2 * rows_all] + sums[2 * rows_all :])
+    center, end = lc[:, L // 2 : L // 2 + 1], lc[:, L - 1 : L]
+    bases = [jnp.zeros((heads, 1), F32)]
     for q in range(chunks):
-        at = slice(q * L, (q + 1) * L)
-        lc = dot(lds[:, at], tri, precision=lax.Precision.HIGHEST)
-        center, end = lc[:, L // 2 : L // 2 + 1], lc[:, L - 1 : L]
-        centers.append(center)
-        ends.append(end)
-        put2(a_s, q, jnp.exp(lc - center))
-        put2(b_s, q, jnp.exp(center - lc) * sts[:, at])
-        put2(e_s, q, jnp.exp(base + lc))
-        base = base + end
+        bases.append(bases[-1] + end[q * heads : (q + 1) * heads])
+    base = bases[-1]
+    put2(a_s, jnp.exp(lc - center))
+    put2(b_s, jnp.exp(center - lc) * st)
+    put2(e_s, jnp.exp(jnp.concatenate(bases[:-1], axis=0) + lc))
+    centers = [center[q * heads : (q + 1) * heads] for q in range(chunks)]
+    ends = [end[q * heads : (q + 1) * heads] for q in range(chunks)]
+
+    pl.semaphore_wait(barrier, chips + 1 + y_count - 1)
+
+    def halo_copies():
+        to = {"ctx": lax.rem(me + 1, n)}
+        tail = pl.ds(tokens - HALO, HALO)
+        return (
+            pltpu.make_async_remote_copy(
+                src_ref=x_ref.at[tail, :], dst_ref=xh, send_sem=halo_send.at[0],
+                recv_sem=halo_recv.at[0], device_id=to, device_id_type=MESH,
+            ),
+            pltpu.make_async_remote_copy(
+                src_ref=bc_ref.at[tail, :], dst_ref=bch, send_sem=halo_send.at[1],
+                recv_sem=halo_recv.at[1], device_id=to, device_id_type=MESH,
+            ),
+        )
+
+    @pl.when(me < n - 1)
+    def _():
+        for copy in halo_copies():
+            copy.start()
+
     lane = iota((heads, 128), 1)
     table = jnp.zeros((heads, 128), F32)
     for q in range(chunks):
@@ -140,33 +173,28 @@
     r_high, r_low = split2(rows[...])
     rowsx[...] = dot(r_high, es[0:heads, :]) + dot(r_low, es[0:heads, :])
 
-    t_all = iota((HALO + tokens, 128), 0) + (first - HALO)
-    m1[...] = jnp.where(crossed(t_all - 1, t_all), 0.0, 1.0)
-    t_all = iota((tokens, 128), 0) + first
-    m2[...] = jnp.where(crossed(t_all - 2, t_all), 0.0, 1.0)
+    def expand_b(i, carry):
+        at = pl.ds(pl.multiple_of(i * 512, 512), 512)
+        xcs[:, at] = dot(b_s[...], es[:, at]).astype(BF16)
+        return carry
+
+    lax.fori_loop(0, width // 512, expand_b, 0)
+
+    def any_of(conditions):
+        hit = conditions[0]
+        for one in conditions[1:]:
+            hit = hit | one
+        return hit
+
+    row8 = iota((8, 128), 0)
+    for r in range(0, HALO + tokens, 8):
+        starts = [d - (first - HALO + r) for d in docs]
+        m1[r : r + 8, :] = jnp.where(any_of([row8 == d for d in starts]), 0.0, 1.0)
+        if r >= HALO:
+            both = [row8 == d for d in starts] + [row8 == d + 1 for d in starts]
+            m2[r - HALO : r - HALO + 8, :] = jnp.where(any_of(both), 0.0, 1.0)
     t_at = iota((L, L), 0)
     s_at = iota((L, L), 1)
-
-    pl.semaphore_wait(barrier, n - 1 + y_count - 1)
-
-    def halo_copies():
-        to = {"ctx": lax.rem(me + 1, n)}
-        tail = pl.ds(tokens - HALO, HALO)
-        return (
-            pltpu.make_async_remote_copy(
-                src_ref=x_ref.at[tail, :], dst_ref=xh, send_sem=halo_send.at[0],
-                recv_sem=halo_recv.at[0], device_id=to, device_id_type=MESH,
-            ),
-            pltpu.make_async_remote_copy(
-                src_ref=bc_ref.at[tail, :], dst_ref=bch, send_sem=halo_send.at[1],
-                recv_sem=halo_recv.at[1], device_id=to, device_id_type=MESH,
-            ),
-        )
-
-    @pl.when(me < n - 1)
-    def _():
-        for copy in halo_copies():
-            copy.start()
 
     small[2].wait()
     small[3].wait()
@@ -187,21 +215,25 @@
 
     taps_bc = cbc_ref[...].astype(F32) * 0.5
 
+    def segment(at):
+        count = 0
+        for d in docs:
+            count = count + jnp.where(at >= d, 1, 0)
+        return count
+
     def shared(q, before):
         block = bcs[q * L : (q + 1) * L, :]
         both = silu_of_half(conv_half(q, block, before, taps_bc))
         b_st, c_st = both[:, :128], both[:, 128:]
-        t_all = t_at + (first + q * L)
-        s_all = s_at + (first + q * L)
+        begin = first + q * L
+        seg_t, seg_s = segment(t_at + begin), segment(iota((1, L), 1) + begin)
         scores = dot(c_st.astype(BF16), b_st.astype(BF16), NT)
-        ok = (s_at <= t_at) & ~crossed(s_all, t_all)
+        ok = (s_at <= t_at) & (seg_t == seg_s)
         gbm[q, 0:L, :] = jnp.where(ok, scores, 0.0).astype(BF16)
-        last = jnp.full((L, L), first + (q + 1) * L - 1, jnp.int32)
-        gbm[q, L : 2 * L, :] = jnp.transpose(jnp.where(crossed(t_all, last), 0.0, b_st)).astype(BF16)
-        begin = jnp.full((L, L), first + q * L, jnp.int32)
-        com[q] = jnp.where(crossed(begin - 1, t_all), 0.0, c_st).astype(BF16)
-        begin = jnp.full((L, L), first, jnp.int32)
-        cam[q * L : (q + 1) * L, :] = jnp.where(crossed(begin - 1, t_all), 0.0, c_st).astype(BF16)
+        b_kept = jnp.where(seg_t == segment(begin + L - 1), b_st, 0.0)
+        gbm[q, L : 2 * L, :] = jnp.transpose(b_kept).astype(BF16)
+        com[q] = jnp.where(seg_t == segment(begin - 1), c_st, 0.0).astype(BF16)
+        cam[q * L : (q + 1) * L, :] = jnp.where(seg_t == segment(first - 1), c_st, 0.0).astype(BF16)
 
     for q in range(1, chunks):
         shared(q, bcs[q * L - HALO : q * L, :])
@@ -218,28 +250,61 @@
 
     shared(0, bch[...])
 
+    def exchange_copy(t):
+        at = pl.ds(t * per_tile, per_tile)
+        return pltpu.make_async_remote_copy(
+            src_ref=sp.at[at, 1 - core], dst_ref=ex.at[at], send_sem=ex_send.at[t],
+            recv_sem=ex_recv.at[t], device_id={"ctx": peer}, device_id_type=MESH,
+        )
+
     def piece_copy(p):
-        owner = p // ppo
         return pltpu.make_async_remote_copy(
-            src_ref=sp.at[p], dst_ref=rp.at[me, lax.rem(p, ppo)], send_sem=send1.at[p],
-            recv_sem=recv1.at[me * ppo + lax.rem(p, ppo)],
-            device_id={"ctx": owner}, device_id_type=MESH,
-        )
+            src_ref=sc.at[p], dst_ref=rp.at[chip, lax.rem(p, ppc)], send_sem=send1.at[p],
+            recv_sem=recv1.at[chip * ppc + lax.rem(p, ppc)],
+            device_id={"ctx": 2 * (p // ppc) + core}, device_id_type=MESH,
+        )
+
+    def keep_of(piece):
+        return piece[64:65, :] + piece[65:66, :]
+
+    def keep_rows(keep):
+        high = keep.astype(BF16).astype(F32)
+        row = iota((KROWS, keep.shape[1]), 0)
+        return jnp.where(row == 0, high, jnp.where(row == 1, keep - high, 0.0)).astype(BF16)
+
+    def both_cores(p):
+        mine, other = sp[p, core].astype(F32), ex[p].astype(F32)
+        return jnp.where(core == 0, mine, other), jnp.where(core == 0, other, mine)
+
+    def give(t):
+        exchange_copy(t).wait_recv()
+        for j in range(per_tile):
+            p = t * per_tile + j
+            early, late = both_cores(p)
+            sc[p, 0:64, :] = (keep_of(late) * early[0:64, :] + late[0:64, :]).astype(BF16)
+            sc[p, 64 : 64 + KROWS, :] = keep_rows(keep_of(late) * keep_of(early))
+
+            @pl.when(p // ppc != chip)
+            def _():
+                piece_copy(p).start()
+
+            @pl.when(p // ppc == chip)
+            def _():
+                rp[chip, lax.rem(p, ppc)] = sc[p]
 
     def pass_a(i, carry):
         t = tile_at(i)
         x_copy(t).wait()
         taps = cx_ref[:, cols(t)].astype(F32) * 0.5
-        etile = es[:, cols(t)]
         state = jnp.zeros((128, W), F32)
-        wide[...] = dot(b_s[...], etile)
         for q in range(chunks):
             at = slice(q * L, (q + 1) * L)
             block = xs[at, cols(t)]
             before = xh[:, cols(t)] if q == 0 else xs[q * L - HALO : q * L, cols(t)]
             xc = silu_of_half(conv_half(q, block, before, taps))
-            xcs[at, cols(t)] = xc.astype(BF16)
-            v = (xc * wide[at, :]).astype(BF16)
+            xc = xc.astype(BF16)
+            v = xc * xcs[at, cols(t)]
+            xcs[at, cols(t)] = xc
             hs[q, :, cols(t)] = state.astype(BF16)
             both = dot(gbm[q], v)
             yl[at, cols(t)] = both[0:L, :]
@@ -249,28 +314,23 @@
                 + rowsx[chunks + q : chunks + q + 1, cols(t)] * fresh
             )
         keep = rowsx[2 * chunks : 2 * chunks + 1, cols(t)]
-        keep_high = keep.astype(BF16).astype(F32)
-        krow = iota((KROWS, W), 0)
-        kblock = jnp.where(
-            krow == 0, keep_high, jnp.where(krow == 1, keep - keep_high, 0.0)
-        ).astype(BF16)
+        krows = keep_rows(keep)
         for j in range(per_tile):
             p = t * per_tile + j
-            lanes = slice((j // 2) * 128, (j // 2) * 128 + 128)
-            sp[p, 0:64, :] = state[(j % 2) * 64 : (j % 2) * 64 + 64, lanes].astype(BF16)
-            sp[p, 64 : 64 + KROWS, :] = kblock[:, lanes]
-
-            @pl.when(p // ppo != me)
-            def _():
-                piece_copy(p).start()
-
-            @pl.when(p // ppo == me)
-            def _():
-                rp[me, lax.rem(p, ppo)] = sp[p]
+            lanes = slice(j * 128, (j + 1) * 128)
+            for half in range(2):
+                sp[p, half, 0:64, :] = state[half * 64 : half * 64 + 64, lanes].astype(BF16)
+                sp[p, half, 64 : 64 + KROWS, :] = krows[:, lanes]
+        exchange_copy(t).start()
+
+        @pl.when(i > 0)
+        def _():
+            give(tile_at(i - 1))
 
         return carry
 
     lax.fori_loop(0, tiles, pass_a, 0)
+    give(tile_at(tiles - 1))
 
     def pass_b(i, carry):
         t = tile_at(i)
@@ -278,12 +338,14 @@
         etile = es[:, cols(t)]
         skip = rowsx[2 * chunks + 1 : 2 * chunks + 2, cols(t)]
         wide[...] = dot(a_s[...], etile)
+        wide2[...] = dot(e_s[...], etile)
         for q in range(chunks):
             at = slice(q * L, (q + 1) * L)
             mixed = yl[at, cols(t)] + dot(com[q], hs[q, :, cols(t)])
             own = mixed * wide[at, :] + skip * xcs[at, cols(t)].astype(F32)
-            yl[at, cols(t)] = own
-            sz[at, cols(t)] = silu_of_half(zs[at, cols(t)].astype(F32) * 0.5)
+            gate = silu_of_half(zs[at, cols(t)].astype(F32) * 0.5)
+            yl[at, cols(t)] = own * gate
+            sz[at, cols(t)] = wide2[at, :] * gate
         return carry
 
     split_b = 3
@@ -291,68 +353,82 @@
 
     def piece_in(d, k):
         return pltpu.make_async_remote_copy(
-            src_ref=sp.at[0], dst_ref=rp.at[d, k], send_sem=send1.at[0],
-            recv_sem=recv1.at[d * ppo + k], device_id={"ctx": me}, device_id_type=MESH,
+            src_ref=sc.at[0], dst_ref=rp.at[d, k], send_sem=send1.at[0],
+            recv_sem=recv1.at[d * ppc + k], device_id={"ctx": peer}, device_id_type=MESH,
         )
 
     def enter_copy(d, k):
         return pltpu.make_async_remote_copy(
-            src_ref=ap.at[d, k], dst_ref=ain.at[me * ppo + k], send_sem=send2.at[d * ppo + k],
-            recv_sem=recv2.at[me * ppo + k], device_id={"ctx": d}, device_id_type=MESH,
+            src_ref=ap.at[d, k], dst_ref=ain.at[chip * ppc + k], send_sem=send2.at[d * ppc + k],
+            recv_sem=recv2.at[chip * ppc + k], device_id={"ctx": 2 * d + core}, device_id_type=MESH,
         )
 
     def enter_in(p):
         return pltpu.make_async_remote_copy(
             src_ref=ap.at[0, 0], dst_ref=ain.at[p], send_sem=send2.at[0],
-            recv_sem=recv2.at[p], device_id={"ctx": p // ppo}, device_id_type=MESH,
-        )
-
-    for k in range(ppo):
+            recv_sem=recv2.at[p], device_id={"ctx": peer}, device_id_type=MESH,
+        )
+
+    for k in range(ppc):
         def scan(d, state):
-            @pl.when(d != me)
+            @pl.when(d != chip)
             def _():
                 piece_in(d, k).wait_recv()
 
             ap[d, k] = state.astype(BF16)
             piece = rp[d, k].astype(F32)
-            return (piece[64:65, :] + piece[65:66, :]) * state + piece[0:64, :]
-
-        lax.fori_loop(0, n, scan, jnp.zeros((64, 128), F32))
+            return keep_of(piece) * state + piece[0:64, :]
+
+        lax.fori_loop(0, chips, scan, jnp.zeros((64, 128), F32))
 
         def spread(i, carry):
-            enter_copy(lax.rem(me + i, n), k).start()
+            enter_copy(lax.rem(chip + chips - i, chips), k).start()
             return carry
 
-        lax.fori_loop(1, n, spread, 0)
-        ain[me * ppo + k] = ap[me, k]
+        lax.fori_loop(1, chips, spread, 0)
+        ain[chip * ppc + k] = ap[chip, k]
 
     lax.fori_loop(split_b, tiles, pass_b, 0)
 
     sq[...] = jnp.zeros_like(sq)
+
+    def forward_copy(t):
+        at = pl.ds(t * per_tile, per_tile)
+        return pltpu.make_async_remote_copy(
+            src_ref=fw.at[at], dst_ref=ent.at[at, own_rows], send_sem=fw_send.at[t],
+            recv_sem=fw_recv.at[t], device_id={"ctx": peer}, device_id_type=MESH,
+        )
+
+    def forward(t):
+        for j in range(per_tile):
+            p = t * per_tile + j
+
+            @pl.when(p // ppc != chip)
+            def _():
+                enter_in(p).wait_recv()
+
+            early, _ = both_cores(p)
+            to_first = ain[p].astype(F32)
+            to_second = keep_of(early) * to_first + early[0:64, :]
+            ent[p, own_rows, :] = jnp.where(core == 0, to_first, to_second).astype(BF16)
+            fw[p] = jnp.where(core == 0, to_second, to_first).astype(BF16)
+        forward_copy(t).start()
+
+    forward(tile_at(0))
 
     def pass_c(i, carry):
         t = tile_at(i)
-        for j in range(per_tile):
-            p = t * per_tile + j
-
-            @pl.when(p // ppo != me)
-            def _():
-                enter_in(p).wait_recv()
-
-        first_piece = t * per_tile
-        entering = jnp.concatenate(
-            [
-                jnp.concatenate([ain[first_piece + 2 * j], ain[first_piece + 2 * j + 1]], axis=0)
-                for j in range(per_tile // 2)
-            ],
-            axis=1,
-        )
-        etile = es[:, cols(t)]
-        wide[...] = dot(e_s[...], etile)
-        wide2[...] = dot(cam[...], entering)
-        for q in range(chunks):
-            at = slice(q * L, (q + 1) * L)
-            gated = (yl[at, cols(t)] + wide2[at, :] * wide[at, :]) * sz[at, cols(t)]
+
+        @pl.when(i + 1 < tiles)
+        def _():
+            forward(tile_at(i + 1))
+
+        forward_copy(t).wait_recv()
+        entering = jnp.concatenate([ent[t * per_tile + j] for j in range(per_tile)], axis=1)
+        step = 2 * L
+        for q in range(tokens // step):
+            at = slice(q * step, (q + 1) * step)
+            gated = yl[at, cols(t)] + dot(cam[at, :], entering) * sz[at, cols(t)]
             g_ref[at, cols(t)] = gated.astype(BF16)
             squares = gated * gated
             sq[at, :] += squares[:, :128] + squares[:, 128:]
@@ -395,20 +471,24 @@
         for copy in halo_copies():
             copy.wait_send()
 
+    for t in range(tiles):
+        exchange_copy(t).wait_send()
+        forward_copy(t).wait_send()
+
     def drain1(p, carry):
-        @pl.when(p // ppo != me)
+        @pl.when(p // ppc != chip)
         def _():
             piece_copy(p).wait_send()
 
         return carry
 
-    lax.fori_loop(0, pieces, drain1, 0)
-    for k in range(ppo):
+    lax.fori_loop(0, pairs, drain1, 0)
+    for k in range(ppc):
         def drain2(i, carry):
-            enter_copy(lax.rem(me + i, n), k).wait_send()
+            enter_copy(lax.rem(chip + chips - i, chips), k).wait_send()
             return carry
 
-        lax.fori_loop(1, n, drain2, 0)
+        lax.fori_loop(1, chips, drain2, 0)
 
 
 def norm_kernel(g_ref, rx_ref, gain_ref, out_ref, stage, sem):
@@ -438,8 +518,8 @@
     tokens, width = x_raw.shape
     heads = log_decay.shape[1]
     chunks, tiles = tokens // L, width // W
-    pieces = 4 * tiles
-    ppo = pieces // n
+    pairs, chips = width // 128, n // 2
+    ppc = pairs // chips
     any_spec = pl.BlockSpec(memory_space=pl.ANY)
     vmem = pl.BlockSpec(memory_space=pltpu.VMEM)
     smem = pl.BlockSpec(memory_space=pltpu.SMEM)
@@ -480,14 +560,19 @@
             pltpu.VMEM((tokens, width), F32),
             pltpu.VMEM((tokens, W), F32),
             pltpu.VMEM((tokens, W), F32),
-            pltpu.VMEM((pieces, 64 + KROWS, 128), BF16),
-            pltpu.VMEM((n, ppo, 64 + KROWS, 128), BF16),
-            pltpu.VMEM((n, ppo, 64, 128), BF16),
-            pltpu.VMEM((pieces, 64, 128), BF16),
+            pltpu.VMEM((pairs, 2, 64 + KROWS, 128), BF16),
+            pltpu.VMEM((pairs, 64 + KROWS, 128), BF16),
+            pltpu.VMEM((pairs, 64 + KROWS, 128), BF16),
+            pltpu.VMEM((chips, ppc, 64 + KROWS, 128), BF16),
+            pltpu.VMEM((chips, ppc, 64, 128), BF16),
+            pltpu.VMEM((pairs, 64, 128), BF16),
+            pltpu.VMEM((pairs, 64, 128), BF16),
+            pltpu.VMEM((pairs, 128, 128), BF16),
             pltpu.VMEM((tokens, 128), F32),
             pltpu.VMEM((y_count, 8, 128), F32),
             dma((6,)), dma((tiles,)), dma((tiles,)), dma((2,)), dma((2,)),
-            dma((pieces,)), dma((pieces,)), dma((pieces,)), dma((pieces,)),
+            dma((tiles,)), dma((tiles,)), dma((pairs,)), dma((pairs,)), dma((pairs,)), dma((pairs,)),
+            dma((tiles,)), dma((tiles,)),
             dma((y_count,)), dma((y_count,)),
         ],
         compiler_params=pltpu.CompilerParams(

time: 45.6 us -> 44.4 us (0.974)
  Pallas kernels: 45.2 us -> 44.2 us
    pallas_call x1, Pallas kernels: 43 us -> 42 us  [per_device(): pl.pallas_call(functools.partial(layer_kernel, n, y_count, float(width *...]
where the time goes in v3:
time: 44.4 us; the launch traced here: 44.2 us
  Pallas kernels  44.2 us (100%)
    pallas_call x1, Pallas kernels, per_device(): pl.pallas_call(functools.partial(layer_kernel, n, y_count, float(width *...  42 us
    pallas_call x1, Pallas kernels, per_device(): pl.pallas_call(norm_kernel, out_shape=jax.ShapeDtypeStruct((tokens, width...  2.25 us

profile of v3, /device:TPU:1, one launch (start us, length us, event | category | flops | bytes accessed | tf_op | source)
XLA Modules:
  0.0 44.2 jit_solution(12352386174908070569)
XLA Ops:
  0.0 0.0 copy-start
  0.0 42.0 %layer.1 = (bf16[1024,2048]{1,0:T(8,128)(2,1)S(1)}, f32[1024,128]{1,0:T(8,128)S(1)}) custom-call(s32[2]{0:T(128)} %docs_ref.1, bf16[1024,2048]{1,0:T(8,128)(2,1)} %x_ref.1, bf16[1024,2048]{1,0:T(8,128)(2,1)} %z_ref.1, bf16[1024,256]{1,0:T(8,128)(2,1)} %bc_ref.1, f32[32,1024]{1,0:T(8,128)} %bitcast.3, f32[32,1024]{1,0:T(8,128)} %bitcast.4, ...), custom_call_target="tpu_custom_call" | custom-call | tf_op jit(solution)/shard_map/layer/pallas_call | solution.py:527
  42.0 0.0 copy-done
  42.0 2.2 %norm.1 = bf16[1024,2048]{1,0:T(8,128)(2,1)} custom-call(bf16[1024,2048]{1,0:T(8,128)(2,1)S(1)} %get-tuple-element.7.g_ref, f32[1024,128]{1,0:T(8,128)S(1)} %get-tuple-element.8.rx_ref, bf16[2048]{0:T(1024)(128)(2,1)S(1)} %copy-done), custom_call_target="tpu_custom_call" | custom-call | tf_op jit(solution)/shard_map/norm/pallas_call | solution.py:586
Async XLA Ops:
  0.0 42.0 %copy-start = (bf16[2048]{0:T(1024)(128)(2,1)S(1)}, bf16[2048]{0:T(1024)(128)(2,1)}, u32[]{:S(2)}) copy-start(bf16[2048]{0:T(1024)(128)(2,1)} %gain_ref.1) | copy-start | bytes 12292

commit v4 on v3

--- a/solution.py
+++ b/solution.py
@@ -11,6 +11,7 @@
 F32, BF16 = jnp.float32, jnp.bfloat16
 L = 128
 W = 256
+UNROLL = 1
 HALO = 16
 KROWS = 16
 NN = (((1,), (0,)), ((), ()))
@@ -32,9 +33,9 @@
 
 def layer_kernel(
     n, y_count, width_all,
-    docs_ref, x_ref, z_ref, bc_ref, ld_ref, st_ref, cx_hbm, cbc_hbm, skip_hbm,
+    docs_hbm, x_ref, z_ref, bc_ref, ld_ref, st_ref, cx_hbm, cbc_hbm, skip_hbm,
     g_ref, rx_ref,
-    xs, zs, bcs, lds, sts, cx_ref, cbc_ref, skip_ref, xh, bch, es, m1, m2, gbm, com, cam, a_s, b_s, e_s, rows, rowsx,
+    docs_ref, xs, zs, bcs, lds, sts, cx_ref, cbc_ref, skip_ref, xh, bch, es, m1, m2, gbm, com, cam, a_s, b_s, e_s, rows, rowsx,
     xcs, hs, yl, sz, wide, wide2, sp, ex, sc, rp, ap, ain, fw, ent, sq, sqx,
     load_sem, x_sem, z_sem, halo_send, halo_recv, ex_send, ex_recv, send1, recv1, send2, recv2,
     fw_send, fw_recv, send3, recv3,
@@ -53,7 +54,6 @@
     own_rows = pl.ds(pl.multiple_of(core * 64, 64), 64)
     hd = width // heads
     first = me * tokens
-    docs = [docs_ref[i] for i in range(docs_ref.shape[0])]
     tile0 = lax.rem(chip * tiles // chips, tiles)
 
     def tile_at(i):
@@ -81,6 +81,7 @@
         greet({"head": lax.rem(my + i, y_count)})
 
     small = [
+        pltpu.make_async_copy(docs_hbm, docs_ref, load_sem.at[6]),
         pltpu.make_async_copy(ld_ref, lds, load_sem.at[0]),
         pltpu.make_async_copy(st_ref, sts, load_sem.at[1]),
         pltpu.make_async_copy(bc_ref, bcs, load_sem.at[2]),
@@ -99,6 +100,9 @@
         (iota((2 * heads, width), 1) // hd) == (iota((2 * heads, width), 0) & (heads - 1)), 1.0, 0.0
     ).astype(BF16)
 
+    small[0].wait()
+    docs = [docs_ref[i] for i in range(docs_ref.shape[0])]
+
     def crossed(low, high):
         hit = None
         for d in docs:
@@ -114,9 +118,22 @@
             both = jnp.concatenate([high[at], low[at]], axis=0)
             ref[q * L : (q + 1) * L, :] = jnp.transpose(both).astype(BF16)
 
-    small[0].wait()
+    def any_of(conditions):
+        hit = conditions[0]
+        for one in conditions[1:]:
+            hit = hit | one
+        return hit
+
+    row8 = iota((8, 128), 0)
+    for r in range(0, HALO + tokens, 8):
+        starts = [d - (first - HALO + r) for d in docs]
+        m1[r : r + 8, :] = jnp.where(any_of([row8 == d for d in starts]), 0.0, 1.0)
+        if r >= HALO:
+            both = [row8 == d for d in starts] + [row8 == d + 1 for d in starts]
+            m2[r - HALO : r - HALO + 8, :] = jnp.where(any_of(both), 0.0, 1.0)
     small[1].wait()
-    small[5].wait()
+    small[2].wait()
+    small[6].wait()
     tri = jnp.where(iota((L, L), 0) <= iota((L, L), 1), 1.0, 0.0).astype(BF16)
     ld = jnp.concatenate([lds[:, q * L : (q + 1) * L] for q in range(chunks)], axis=0)
     st = jnp.concatenate([sts[:, q * L : (q + 1) * L] for q in range(chunks)], axis=0)
@@ -180,25 +197,12 @@
 
     lax.fori_loop(0, width // 512, expand_b, 0)
 
-    def any_of(conditions):
-        hit = conditions[0]
-        for one in conditions[1:]:
-            hit = hit | one
-        return hit
-
-    row8 = iota((8, 128), 0)
-    for r in range(0, HALO + tokens, 8):
-        starts = [d - (first - HALO + r) for d in docs]
-        m1[r : r + 8, :] = jnp.where(any_of([row8 == d for d in starts]), 0.0, 1.0)
-        if r >= HALO:
-            both = [row8 == d for d in starts] + [row8 == d + 1 for d in starts]
-            m2[r - HALO : r - HALO + 8, :] = jnp.where(any_of(both), 0.0, 1.0)
     t_at = iota((L, L), 0)
     s_at = iota((L, L), 1)
 
-    small[2].wait()
     small[3].wait()
     small[4].wait()
+    small[5].wait()
 
     def conv_half(q, block, before, taps):
         ext = jnp.concatenate([before, block], axis=0).astype(F32)
@@ -292,8 +296,7 @@
             def _():
                 rp[chip, lax.rem(p, ppc)] = sc[p]
 
-    def pass_a(i, carry):
-        t = tile_at(i)
+    def tile_a(t):
         x_copy(t).wait()
         taps = cx_ref[:, cols(t)].astype(F32) * 0.5
         state = jnp.zeros((128, W), F32)
@@ -321,16 +324,22 @@
             for half in range(2):
                 sp[p, half, 0:64, :] = state[half * 64 : half * 64 + 64, lanes].astype(BF16)
                 sp[p, half, 64 : 64 + KROWS, :] = krows[:, lanes]
-        exchange_copy(t).start()
+
+    def pass_a(i, carry):
+        at = [tile_at(UNROLL * i + j) for j in range(UNROLL)]
+        for t in at:
+            tile_a(t)
+        for t in at:
+            exchange_copy(t).start()
 
         @pl.when(i > 0)
         def _():
-            give(tile_at(i - 1))
+            for j in range(UNROLL):
+                give(tile_at(UNROLL * (i - 1) + j))
 
         return carry
 
-    lax.fori_loop(0, tiles, pass_a, 0)
-    give(tile_at(tiles - 1))
+    lax.fori_loop(0, tiles // UNROLL, pass_a, 0)
 
     def pass_b(i, carry):
         t = tile_at(i)
@@ -348,8 +357,11 @@
             sz[at, cols(t)] = wide2[at, :] * gate
         return carry
 
+    lax.fori_loop(0, 1, pass_b, 0)
+    for j in range(UNROLL):
+        give(tile_at(tiles - UNROLL + j))
     split_b = 3
-    lax.fori_loop(0, split_b, pass_b, 0)
+    lax.fori_loop(1, split_b, pass_b, 0)
 
     def piece_in(d, k):
         return pltpu.make_async_remote_copy(
@@ -370,16 +382,16 @@
         )
 
     for k in range(ppc):
-        def scan(d, state):
+        for d in range(chips):
             @pl.when(d != chip)
             def _():
                 piece_in(d, k).wait_recv()
 
+        state = jnp.zeros((64, 128), F32)
+        for d in range(chips):
             ap[d, k] = state.astype(BF16)
             piece = rp[d, k].astype(F32)
-            return keep_of(piece) * state + piece[0:64, :]
-
-        lax.fori_loop(0, chips, scan, jnp.zeros((64, 128), F32))
+            state = keep_of(piece) * state + piece[0:64, :]
 
         def spread(i, carry):
             enter_copy(lax.rem(chip + chips - i, chips), k).start()
@@ -414,16 +426,10 @@
             fw[p] = jnp.where(core == 0, to_second, to_first).astype(BF16)
         forward_copy(t).start()
 
-    forward(tile_at(0))
-
-    def pass_c(i, carry):
-        t = tile_at(i)
-
-        @pl.when(i + 1 < tiles)
-        def _():
-            forward(tile_at(i + 1))
-
-        forward_copy(t).wait_recv()
+    for j in range(UNROLL):
+        forward(tile_at(j))
+
+    def tile_c(t):
         entering = jnp.concatenate([ent[t * per_tile + j] for j in range(per_tile)], axis=1)
         step = 2 * L
         for q in range(tokens // step):
@@ -432,9 +438,21 @@
             g_ref[at, cols(t)] = gated.astype(BF16)
             squares = gated * gated
             sq[at, :] += squares[:, :128] + squares[:, 128:]
+
+    def pass_c(i, carry):
+        for j in range(UNROLL):
+            @pl.when(UNROLL * (i + 1) + j < tiles)
+            def _():
+                forward(tile_at(UNROLL * (i + 1) + j))
+
+        at = [tile_at(UNROLL * i + j) for j in range(UNROLL)]
+        for t in at:
+            forward_copy(t).wait_recv()
+        for t in at:
+            tile_c(t)
         return carry
 
-    lax.fori_loop(0, tiles, pass_c, 0)
+    lax.fori_loop(0, tiles // UNROLL, pass_c, 0)
 
     total = jnp.zeros((8, L), F32)
     for q in range(chunks):
@@ -522,7 +540,6 @@
     ppc = pairs // chips
     any_spec = pl.BlockSpec(memory_space=pl.ANY)
     vmem = pl.BlockSpec(memory_space=pltpu.VMEM)
-    smem = pl.BlockSpec(memory_space=pltpu.SMEM)
     dma = pltpu.SemaphoreType.DMA
     gated, scale = pl.pallas_call(
         functools.partial(layer_kernel, n, y_count, float(width * y_count)),
@@ -530,9 +547,10 @@
             pltpu.VMEM((tokens, width), BF16),
             pltpu.VMEM((tokens, 128), F32),
         ),
-        in_specs=[smem] + [any_spec] * 8,
+        in_specs=[any_spec] * 9,
         out_specs=(vmem, vmem),
         scratch_shapes=[
+            pltpu.SMEM(doc_starts.shape, jnp.int32),
             pltpu.VMEM((tokens, width), BF16),
             pltpu.VMEM((tokens, width), BF16),
             pltpu.VMEM((tokens, 256), BF16),
@@ -570,7 +588,7 @@
             pltpu.VMEM((pairs, 128, 128), BF16),
             pltpu.VMEM((tokens, 128), F32),
             pltpu.VMEM((y_count, 8, 128), F32),
-            dma((6,)), dma((tiles,)), dma((tiles,)), dma((2,)), dma((2,)),
+            dma((7,)), dma((tiles,)), dma((tiles,)), dma((2,)), dma((2,)),
             dma((tiles,)), dma((tiles,)), dma((pairs,)), dma((pairs,)), dma((pairs,)), dma((pairs,)),
             dma((tiles,)), dma((tiles,)),
             dma((y_count,)), dma((y_count,)),

time: 44.4 us -> 43.5 us (0.980)
  Pallas kernels: 44.2 us -> 43.3 us
    pallas_call x1, Pallas kernels: 42 us -> 41.1 us  [per_device(): pl.pallas_call(functools.partial(layer_kernel, n, y_count, float(width *...]
where the time goes in v4:
time: 43.5 us; the launch traced here: 43.4 us
  Pallas kernels  43.3 us (100%)
    pallas_call x1, Pallas kernels, per_device(): pl.pallas_call(functools.partial(layer_kernel, n, y_count, float(width *...  41.1 us
    pallas_call x1, Pallas kernels, per_device(): pl.pallas_call(norm_kernel, out_shape=jax.ShapeDtypeStruct((tokens, width...  2.25 us

profile of v4, /device:TPU:1, one launch (start us, length us, event | category | flops | bytes accessed | tf_op | source)
XLA Modules:
  0.0 43.4 jit_solution(1720782861892724670)
XLA Ops:
  0.0 0.0 copy-start
  0.0 41.1 %layer.1 = (bf16[1024,2048]{1,0:T(8,128)(2,1)S(1)}, f32[1024,128]{1,0:T(8,128)S(1)}) custom-call(s32[2]{0:T(128)} %docs_hbm.1, bf16[1024,2048]{1,0:T(8,128)(2,1)} %x_ref.1, bf16[1024,2048]{1,0:T(8,128)(2,1)} %z_ref.1, bf16[1024,256]{1,0:T(8,128)(2,1)} %bc_ref.1, f32[32,1024]{1,0:T(8,128)} %bitcast.3, f32[32,1024]{1,0:T(8,128)} %bitcast.4, ...), custom_call_target="tpu_custom_call" | custom-call | tf_op jit(solution)/shard_map/layer/pallas_call | solution.py:544
  41.1 0.0 copy-done
  41.1 2.2 %norm.1 = bf16[1024,2048]{1,0:T(8,128)(2,1)} custom-call(bf16[1024,2048]{1,0:T(8,128)(2,1)S(1)} %get-tuple-element.7.g_ref, f32[1024,128]{1,0:T(8,128)S(1)} %get-tuple-element.8.rx_ref, bf16[2048]{0:T(1024)(128)(2,1)S(1)} %copy-done), custom_call_target="tpu_custom_call" | custom-call | tf_op jit(solution)/shard_map/norm/pallas_call | solution.py:604
Async XLA Ops:
  0.0 41.1 %copy-start = (bf16[2048]{0:T(1024)(128)(2,1)S(1)}, bf16[2048]{0:T(1024)(128)(2,1)}, u32[]{:S(2)}) copy-start(bf16[2048]{0:T(1024)(128)(2,1)} %gain_ref.1) | copy-start | bytes 12292

commit v5 on v4

--- a/solution.py
+++ b/solution.py
@@ -11,6 +11,8 @@
 F32, BF16 = jnp.float32, jnp.bfloat16
 L = 128
 W = 256
+SECOND = 7
+AHEAD = 3
 UNROLL = 1
 HALO = 16
 KROWS = 16
@@ -400,7 +402,6 @@
         lax.fori_loop(1, chips, spread, 0)
         ain[chip * ppc + k] = ap[chip, k]
 
-    lax.fori_loop(split_b, tiles, pass_b, 0)
 
     sq[...] = jnp.zeros_like(sq)
 
@@ -425,9 +426,6 @@
             ent[p, own_rows, :] = jnp.where(core == 0, to_first, to_second).astype(BF16)
             fw[p] = jnp.where(core == 0, to_second, to_first).astype(BF16)
         forward_copy(t).start()
-
-    for j in range(UNROLL):
-        forward(tile_at(j))
 
     def tile_c(t):
         entering = jnp.concatenate([ent[t * per_tile + j] for j in range(per_tile)], axis=1)
@@ -440,10 +438,9 @@
             sq[at, :] += squares[:, :128] + squares[:, 128:]
 
     def pass_c(i, carry):
-        for j in range(UNROLL):
-            @pl.when(UNROLL * (i + 1) + j < tiles)
-            def _():
-                forward(tile_at(UNROLL * (i + 1) + j))
+        @pl.when(i + AHEAD < tiles)
+        def _():
+            forward(tile_at(i + AHEAD))
 
         at = [tile_at(UNROLL * i + j) for j in range(UNROLL)]
         for t in at:
@@ -452,6 +449,13 @@
             tile_c(t)
         return carry
 
+    def forward_step(i, carry):
+        forward(tile_at(i))
+        return carry
+
+    lax.fori_loop(split_b, SECOND, pass_b, 0)
+    lax.fori_loop(0, AHEAD, forward_step, 0)
+    lax.fori_loop(SECOND, tiles, pass_b, 0)
     lax.fori_loop(0, tiles // UNROLL, pass_c, 0)
 
     total = jnp.zeros((8, L), F32)

time: 43.5 us -> 42.1 us (0.968)
  Pallas kernels: 43.3 us -> 42 us
    pallas_call x1, Pallas kernels: 41.1 us -> 39.8 us  [per_device(): pl.pallas_call(functools.partial(layer_kernel, n, y_count, float(width *...]
where the time goes in v5:
time: 42.1 us; the launch traced here: 42 us
  Pallas kernels  42 us (100%)
    pallas_call x1, Pallas kernels, per_device(): pl.pallas_call(functools.partial(layer_kernel, n, y_count, float(width *...  39.8 us
    pallas_call x1, Pallas kernels, per_device(): pl.pallas_call(norm_kernel, out_shape=jax.ShapeDtypeStruct((tokens, width...  2.25 us

profile of v5, /device:TPU:1, one launch (start us, length us, event | category | flops | bytes accessed | tf_op | source)
XLA Modules:
  0.0 42.0 jit_solution(6976790153166987462)
XLA Ops:
  0.0 0.0 copy-start
  0.0 39.8 %layer.1 = (bf16[1024,2048]{1,0:T(8,128)(2,1)S(1)}, f32[1024,128]{1,0:T(8,128)S(1)}) custom-call(s32[2]{0:T(128)} %docs_hbm.1, bf16[1024,2048]{1,0:T(8,128)(2,1)} %x_ref.1, bf16[1024,2048]{1,0:T(8,128)(2,1)} %z_ref.1, bf16[1024,256]{1,0:T(8,128)(2,1)} %bc_ref.1, f32[32,1024]{1,0:T(8,128)} %bitcast.3, f32[32,1024]{1,0:T(8,128)} %bitcast.4, ...), custom_call_target="tpu_custom_call" | custom-call | tf_op jit(solution)/shard_map/layer/pallas_call | solution.py:548
  39.8 0.0 copy-done
  39.8 2.2 %norm.1 = bf16[1024,2048]{1,0:T(8,128)(2,1)} custom-call(bf16[1024,2048]{1,0:T(8,128)(2,1)S(1)} %get-tuple-element.7.g_ref, f32[1024,128]{1,0:T(8,128)S(1)} %get-tuple-element.8.rx_ref, bf16[2048]{0:T(1024)(128)(2,1)S(1)} %copy-done), custom_call_target="tpu_custom_call" | custom-call | tf_op jit(solution)/shard_map/norm/pallas_call | solution.py:608
Async XLA Ops:
  0.0 39.8 %copy-start = (bf16[2048]{0:T(1024)(128)(2,1)S(1)}, bf16[2048]{0:T(1024)(128)(2,1)}, u32[]{:S(2)}) copy-start(bf16[2048]{0:T(1024)(128)(2,1)} %gain_ref.1) | copy-start | bytes 12292

commit v6 on v5

--- a/solution.py
+++ b/solution.py
@@ -95,8 +95,6 @@
         copy.start()
     for i in range(tiles):
         x_copy(tile_at(i)).start()
-    for i in range(tiles):
-        z_copy(tile_at(i)).start()
 
     es[...] = jnp.where(
         (iota((2 * heads, width), 1) // hd) == (iota((2 * heads, width), 0) & (heads - 1)), 1.0, 0.0
@@ -175,6 +173,9 @@
     def _():
         for copy in halo_copies():
             copy.start()
+
+    for i in range(tiles):
+        z_copy(tile_at(i)).start()
 
     lane = iota((heads, 128), 1)
     table = jnp.zeros((heads, 128), F32)

time: 42.1 us -> 41.5 us (0.986)
  Pallas kernels: 42 us -> 41.4 us
    pallas_call x1, Pallas kernels: 39.8 us -> 39.1 us  [per_device(): pl.pallas_call(functools.partial(layer_kernel, n, y_count, float(width *...]
where the time goes in v6:
time: 41.5 us; the launch traced here: 41.4 us
  Pallas kernels  41.4 us (100%)
    pallas_call x1, Pallas kernels, per_device(): pl.pallas_call(functools.partial(layer_kernel, n, y_count, float(width *...  39.1 us
    pallas_call x1, Pallas kernels, per_device(): pl.pallas_call(norm_kernel, out_shape=jax.ShapeDtypeStruct((tokens, width...  2.25 us

profile of v6, /device:TPU:1, one launch (start us, length us, event | category | flops | bytes accessed | tf_op | source)
XLA Modules:
  0.0 41.4 jit_solution(8255451303435337740)
XLA Ops:
  0.0 0.0 copy-start
  0.0 39.1 %layer.1 = (bf16[1024,2048]{1,0:T(8,128)(2,1)S(1)}, f32[1024,128]{1,0:T(8,128)S(1)}) custom-call(s32[2]{0:T(128)} %docs_hbm.1, bf16[1024,2048]{1,0:T(8,128)(2,1)} %x_ref.1, bf16[1024,2048]{1,0:T(8,128)(2,1)} %z_ref.1, bf16[1024,256]{1,0:T(8,128)(2,1)} %bc_ref.1, f32[32,1024]{1,0:T(8,128)} %bitcast.3, f32[32,1024]{1,0:T(8,128)} %bitcast.4, ...), custom_call_target="tpu_custom_call" | custom-call | tf_op jit(solution)/shard_map/layer/pallas_call | solution.py:549
  39.1 0.0 copy-done
  39.1 2.2 %norm.1 = bf16[1024,2048]{1,0:T(8,128)(2,1)} custom-call(bf16[1024,2048]{1,0:T(8,128)(2,1)S(1)} %get-tuple-element.7.g_ref, f32[1024,128]{1,0:T(8,128)S(1)} %get-tuple-element.8.rx_ref, bf16[2048]{0:T(1024)(128)(2,1)S(1)} %copy-done), custom_call_target="tpu_custom_call" | custom-call | tf_op jit(solution)/shard_map/norm/pallas_call | solution.py:609
Async XLA Ops:
  0.0 39.1 %copy-start = (bf16[2048]{0:T(1024)(128)(2,1)S(1)}, bf16[2048]{0:T(1024)(128)(2,1)}, u32[]{:S(2)}) copy-start(bf16[2048]{0:T(1024)(128)(2,1)} %gain_ref.1) | copy-start | bytes 12292
